TPU v7x, 256 devices: a whole 4x4x8 slice. The times are simulated.
256 devices in a mesh: dp: 8 (over z), ulysses: 32 (over y, x, core).
Axes of the slice: x: 4, y: 4, z: 8, core: 2. Of those that a mesh axis runs over, the one named last changes fastest.
Arguments:
- q_raw: bfloat16 [8, 4096, 3072], P('dp', 'ulysses')
- k_raw: bfloat16 [8, 4096, 3072], P('dp', 'ulysses')
- values: bfloat16 [8, 4096, 3072], P('dp', 'ulysses'), may hold values from -6 to 6
- grad_out: bfloat16 [8, 4096, 3072], P('dp', 'ulysses'), may hold values from -6 to 6
- q_gain: float32 [128], replicated
- k_gain: float32 [128], replicated
- block_masks: int32 [24, 32, 32], replicated, may hold values from 0 to 1, as said below
Outputs:
- grad_q_raw: bfloat16 [8, 4096, 3072], P('dp', 'ulysses')
- grad_k_raw: bfloat16 [8, 4096, 3072], P('dp', 'ulysses')
- grad_values: bfloat16 [8, 4096, 3072], P('dp', 'ulysses')
- gain_grads: float32 [2, 128], replicated
Inputs may be any that keep to these rules, and one draw needn't show every extreme that they name: `block_masks`: every diagonal block is 1. A third of the heads are dense with some blocks missing, a third keep a band of neighbouring blocks, a third keep blocks a fixed stride apart; which heads are which is drawn.
All inputs are finite; a program needn't handle non-finite values.
Results may differ from a plain program's by a relative error of at most 0.0045.
The roundings to bfloat16 on the way count: a program that leaves them out, or rounds other values in their place, can miss the bound.
Values may be sent and summed in bfloat16 or wider, within the bound.
No kernel may reach another device: no remote copies, remote signals or barrier semaphores. Data moves between devices by JAX's collectives and lax.ppermute only.
A program may use at most 64 MiB of HBM per device.

v0:
```python
import jax
import jax.numpy as jnp
from jax import lax
from jax.sharding import PartitionSpec as P

HEADS = 24
HEAD_DIM = 128
SPLITS = 8
BLOCK = 128
TILE = 512
ITEMS = 32


norm_eps = 1e-06
neg_fill = -1e30


def rms_norm(raw, gain):
    raw_float = raw.astype(jnp.float32)
    spread = jnp.sqrt(jnp.mean(raw_float * raw_float, axis=-1, keepdims=True) + norm_eps)
    return (raw_float, spread, (raw_float / spread * gain).astype(jnp.bfloat16))


def norm_back(raw_float, spread, gain, grad_normed):
    inner = jnp.sum(gain * grad_normed * raw_float, axis=-1, keepdims=True)
    return gain * grad_normed / spread - raw_float * inner / (HEAD_DIM * spread**3)


def dot_rows(left_side, right_side):
    return lax.dot_general(
        left_side, right_side, (((1,), (1,)), ((), ())), preferred_element_type=jnp.float32
    )


def dot_cols(left_side, right_side):
    return lax.dot_general(
        left_side, right_side, (((0,), (0,)), ((), ())), preferred_element_type=jnp.float32
    )


def rows_of(source, tile_index):
    return lax.dynamic_slice_in_dim(source, tile_index * TILE, TILE, 0)


def add_rows(target, addend, tile_index):
    return lax.dynamic_update_slice_in_dim(
        target, rows_of(target, tile_index) + addend, tile_index * TILE, 0
    )


def item_grads(columns, mask_head, half_code, q_gain, k_gain):
    seq_len = columns.shape[0]
    q_float, q_spread, q_normed = rms_norm(columns[:, :HEAD_DIM], q_gain)
    k_float, k_spread, k_normed = rms_norm(columns[:, HEAD_DIM : 2 * HEAD_DIM], k_gain)
    v_rows = columns[:, 2 * HEAD_DIM : 3 * HEAD_DIM]
    o_grads = columns[:, 3 * HEAD_DIM :]
    tile_count = seq_len // TILE
    tile_blocks = TILE // BLOCK
    active = (
        jnp.max(mask_head.reshape(tile_count, tile_blocks, tile_count, tile_blocks), axis=(1, 3))
        > 0
    )
    first_tile = jnp.where(half_code == 2, tile_count // 2, 0)
    last_tile = jnp.where(half_code == 1, tile_count // 2, tile_count)
    score_scale = HEAD_DIM ** (-0.5)

    def allowed_at(row_tile, col_tile):
        blocks = lax.dynamic_slice(
            mask_head, (row_tile * tile_blocks, col_tile * tile_blocks), (tile_blocks, tile_blocks)
        )
        return jnp.repeat(jnp.repeat(blocks, BLOCK, 0), BLOCK, 1) > 0

    def query_tile(row_tile, carry):
        grad_qn, grad_kn, grad_v = carry
        q_tile = rows_of(q_normed, row_tile)
        o_tile = rows_of(o_grads, row_tile)

        def stats_step(col_tile, stats):

            def stats_visit(stats_in):
                run_max, run_sum, run_dot = stats_in
                allowed = allowed_at(row_tile, col_tile)
                scores = jnp.where(
                    allowed, dot_rows(q_tile, rows_of(k_normed, col_tile)) * score_scale, neg_fill
                )
                grad_weights = dot_rows(o_tile, rows_of(v_rows, col_tile))
                new_max = jnp.maximum(run_max, jnp.max(scores, axis=1, keepdims=True))
                weights = jnp.where(allowed, jnp.exp(scores - new_max), 0.0)
                rescale = jnp.exp(run_max - new_max)
                return (
                    new_max,
                    run_sum * rescale + jnp.sum(weights, axis=1, keepdims=True),
                    run_dot * rescale + jnp.sum(weights * grad_weights, axis=1, keepdims=True),
                )

            return lax.cond(
                active[row_tile, col_tile], stats_visit, lambda unchanged: unchanged, stats
            )

        start = (
            jnp.full((TILE, 1), neg_fill, jnp.float32),
            jnp.zeros((TILE, 1), jnp.float32),
            jnp.zeros((TILE, 1), jnp.float32),
        )
        run_max, run_sum, run_dot = lax.fori_loop(0, tile_count, stats_step, start)
        log_total = run_max + jnp.log(run_sum)
        row_delta = run_dot / run_sum

        def grad_step(col_tile, inner):

            def grad_visit(inner_in):
                tile_dq, grad_keys, grad_vals = inner_in
                allowed = allowed_at(row_tile, col_tile)
                k_tile = rows_of(k_normed, col_tile)
                v_tile = rows_of(v_rows, col_tile)
                scores = jnp.where(allowed, dot_rows(q_tile, k_tile) * score_scale, neg_fill)
                weights = jnp.where(allowed, jnp.exp(scores - log_total), 0.0)
                grad_weights = dot_rows(o_tile, v_tile)
                grad_scores = weights * (grad_weights - row_delta)
                weights_half = weights.astype(jnp.bfloat16)
                scores_half = grad_scores.astype(jnp.bfloat16)
                tile_dq = (
                    tile_dq
                    + jnp.dot(scores_half, k_tile, preferred_element_type=jnp.float32) * score_scale
                )
                grad_keys = add_rows(
                    grad_keys, dot_cols(scores_half, q_tile) * score_scale, col_tile
                )
                grad_vals = add_rows(grad_vals, dot_cols(weights_half, o_tile), col_tile)
                return (tile_dq, grad_keys, grad_vals)

            return lax.cond(
                active[row_tile, col_tile], grad_visit, lambda unchanged: unchanged, inner
            )

        tile_dq, grad_kn, grad_v = lax.fori_loop(
            0, tile_count, grad_step, (jnp.zeros((TILE, HEAD_DIM), jnp.float32), grad_kn, grad_v)
        )
        grad_qn = lax.dynamic_update_slice_in_dim(grad_qn, tile_dq, row_tile * TILE, 0)
        return (grad_qn, grad_kn, grad_v)

    empty = jnp.zeros((seq_len, HEAD_DIM), jnp.float32)
    grad_qn, grad_kn, grad_v = lax.fori_loop(
        first_tile, last_tile, query_tile, (empty, empty, empty)
    )
    grad_q = norm_back(q_float, q_spread, q_gain, grad_qn)
    grad_k = norm_back(k_float, k_spread, k_gain, grad_kn)
    gain_part = jnp.stack(
        [
            jnp.sum(grad_qn * q_float / q_spread, axis=0),
            jnp.sum(grad_kn * k_float / k_spread, axis=0),
        ]
    )
    return (jnp.concatenate([grad_q, grad_k, grad_v], axis=1), gain_part)


def body(q_raw, k_raw, values, grad_out, q_gain, k_gain, block_masks):
    unit_count = lax.axis_size("ulysses")
    group_count = lax.axis_size("dp")
    device_rank = lax.axis_index("ulysses")
    videos_here, tok_rows, width = q_raw.shape
    seq_len = tok_rows * unit_count
    per_unit = ITEMS // unit_count
    counter = jnp.arange(ITEMS, dtype=jnp.int32)
    paired = counter < 2 * SPLITS
    item_heads = jnp.where(paired, counter // 2, counter - SPLITS)
    item_halves = jnp.where(paired, 1 + counter % 2, 0)
    stacked = jnp.concatenate(
        [
            operand.reshape(videos_here, tok_rows, HEADS, HEAD_DIM)
            for operand in (q_raw, k_raw, values, grad_out)
        ],
        axis=3,
    )
    picked = jnp.take(stacked, item_heads, axis=2)
    outgoing = picked.transpose(2, 0, 1, 3).reshape(
        unit_count, per_unit, videos_here, tok_rows, 4 * HEAD_DIM
    )
    arrived = lax.all_to_all(outgoing, "ulysses", split_axis=0, concat_axis=3, tiled=True)
    item_index = device_rank * per_unit + 0
    head_index = item_heads[item_index]
    half_code = item_halves[item_index]
    mask_head = lax.dynamic_index_in_dim(block_masks, head_index, 0, keepdims=False)
    item_grad, gain_part = item_grads(arrived[0, 0, 0], mask_head, half_code, q_gain, k_gain)
    video_rows = [item_grad]
    results = [jnp.stack(video_rows)]
    backward = jnp.stack(results)[None]
    returned = lax.all_to_all(
        backward.astype(jnp.bfloat16), "ulysses", split_axis=3, concat_axis=0, tiled=True
    ).astype(backward.dtype)
    returned = returned.reshape(ITEMS, videos_here, tok_rows, 3 * HEAD_DIM)
    selector = (item_heads[:, None] == jnp.arange(HEADS)[None, :]).astype(jnp.float32)
    merged = jnp.einsum("ih,ivtc->vthc", selector, returned, precision=lax.Precision.HIGHEST)
    grad_q_raw = merged[..., :HEAD_DIM].reshape(videos_here, tok_rows, width).astype(jnp.bfloat16)
    grad_k_raw = (
        merged[..., HEAD_DIM : 2 * HEAD_DIM]
        .reshape(videos_here, tok_rows, width)
        .astype(jnp.bfloat16)
    )
    grad_values = (
        merged[..., 2 * HEAD_DIM :].reshape(videos_here, tok_rows, width).astype(jnp.bfloat16)
    )
    summed = lax.psum(gain_part, ("dp", "ulysses"))
    gain_grads = summed * (group_count * videos_here * seq_len * HEADS) ** (-0.5)
    return (grad_q_raw, grad_k_raw, grad_values, gain_grads)


def solution(mesh):
    return jax.shard_map(
        body,
        mesh=mesh,
        in_specs=(
            P("dp", "ulysses", None),
            P("dp", "ulysses", None),
            P("dp", "ulysses", None),
            P("dp", "ulysses", None),
            P(),
            P(),
            P(),
        ),
        out_specs=(
            P("dp", "ulysses", None),
            P("dp", "ulysses", None),
            P("dp", "ulysses", None),
            P(),
        ),
        check_vma=False,
    )
```

profile of v0, /device:TPU:1, one launch (start us, length us, event | category | flops | bytes accessed | tf_op | source)
XLA Modules:
  0.0 979.9 jit_solution(11432165889519738224)
XLA Ops:
  25.1 8.6 all-to-all-start
  38.6 45.4 %all-to-all-done = bf16[32,1,1,128,512]{4,3,2,1,0:T(8,128)(2,1)} async-done(((bf16[32,1,1,128,512]{4,3,2,1,0:T(8,128)(2,1)}), bf16[32,1,1,128,512]{4,3,2,1,0:T(8,128)(2,1)}, u32[]{:S(2)}, u32[]{:S(2)}) %all-to-all-start) | async-done | bytes 4194336 | tf_op jit(solution)/shard_map/all_to_all | solution.py:179
  98.4 293.6 %while.54 = (s32[]{:T(128)}, f32[4096,128]{1,0:T(8,128)}, f32[4096,128]{1,0:T(8,128)}, f32[4096,128]{1,0:T(8,128)}, s32[]{:T(128)}, /*index=5*/bf16[4096,128]{1,...) while((s32[]{:T(128)}, f32[4096,128]{1,0:T(8,128)}, ...), condition=%wide.region_15.16_spmd, body=%wide.region_3.15_spmd.sunk | while | flops 474286656 | bytes 13313613 | solution.py:143
  99.5 19.7 %while.55 = (s32[]{:T(128)}, f32[512,1]{0,1:T(1,128)S(1)}, f32[512,1]{0,1:T(1,128)S(1)}, f32[512,1]{0,1:T(1,128)S(1)}, pred[8,8]{1,0:T(8,128)(4,1)S(1)}, /*index...) while((s32[]{:T(128)}, f32[512,1]{0,1:T(1,128)S(1)}, ...), condition=%wide.region_10.10_spmd, body=%wide.region_4.9_spmd.sunk | while | flops 136316448 | bytes 4764170 | solution.py:105
  119.2 51.8 %while.56 = (s32[]{:T(128)}, f32[512,128]{1,0:T(8,128)S(1)}, f32[4096,128]{1,0:T(8,128)}, f32[4096,128]{1,0:T(8,128)}, pred[8,8]{1,0:T(8,128)(4,1)S(1)}, /*index...) while((s32[]{:T(128)}, f32[512,128]{1,0:T(8,128)S(1)}, ...), condition=%wide.region_14.14_spmd, body=%wide.region_11.13_spmd.sunk | while | flops 337969184 | bytes 7221814 | solution.py:136
  120.5 5.2 conditional.5
  127.0 5.2 conditional.5
  133.5 5.2 conditional.5
  140.0 5.2 conditional.5
  146.5 5.2 conditional.5
  159.4 5.2 conditional.5
  165.8 5.2 conditional.5
  172.8 19.7 %while.55 = (s32[]{:T(128)}, f32[512,1]{0,1:T(1,128)S(1)}, f32[512,1]{0,1:T(1,128)S(1)}, f32[512,1]{0,1:T(1,128)S(1)}, pred[8,8]{1,0:T(8,128)(4,1)S(1)}, /*index...) while((s32[]{:T(128)}, f32[512,1]{0,1:T(1,128)S(1)}, ...), condition=%wide.region_10.10_spmd, body=%wide.region_4.9_spmd.sunk | while | flops 136316448 | bytes 4764170 | solution.py:105
  192.6 51.8 %while.56 = (s32[]{:T(128)}, f32[512,128]{1,0:T(8,128)S(1)}, f32[4096,128]{1,0:T(8,128)}, f32[4096,128]{1,0:T(8,128)}, pred[8,8]{1,0:T(8,128)(4,1)S(1)}, /*index...) while((s32[]{:T(128)}, f32[512,128]{1,0:T(8,128)S(1)}, ...), condition=%wide.region_14.14_spmd, body=%wide.region_11.13_spmd.sunk | while | flops 337969184 | bytes 7221814 | solution.py:136
  193.9 5.2 conditional.5
  200.4 5.2 conditional.5
  206.9 5.2 conditional.5
  213.4 5.2 conditional.5
  219.9 5.2 conditional.5
  232.8 5.2 conditional.5
  239.2 5.2 conditional.5
  246.2 19.7 %while.55 = (s32[]{:T(128)}, f32[512,1]{0,1:T(1,128)S(1)}, f32[512,1]{0,1:T(1,128)S(1)}, f32[512,1]{0,1:T(1,128)S(1)}, pred[8,8]{1,0:T(8,128)(4,1)S(1)}, /*index...) while((s32[]{:T(128)}, f32[512,1]{0,1:T(1,128)S(1)}, ...), condition=%wide.region_10.10_spmd, body=%wide.region_4.9_spmd.sunk | while | flops 136316448 | bytes 4764170 | solution.py:105
  266.0 51.8 %while.56 = (s32[]{:T(128)}, f32[512,128]{1,0:T(8,128)S(1)}, f32[4096,128]{1,0:T(8,128)}, f32[4096,128]{1,0:T(8,128)}, pred[8,8]{1,0:T(8,128)(4,1)S(1)}, /*index...) while((s32[]{:T(128)}, f32[512,128]{1,0:T(8,128)S(1)}, ...), condition=%wide.region_14.14_spmd, body=%wide.region_11.13_spmd.sunk | while | flops 337969184 | bytes 7221814 | solution.py:136
  267.3 5.2 conditional.5
  273.8 5.2 conditional.5
  280.2 5.2 conditional.5
  286.7 5.2 conditional.5
  293.2 5.2 conditional.5
  299.7 5.2 conditional.5
  306.2 5.2 conditional.5
  312.6 5.2 conditional.5
  319.6 19.7 %while.55 = (s32[]{:T(128)}, f32[512,1]{0,1:T(1,128)S(1)}, f32[512,1]{0,1:T(1,128)S(1)}, f32[512,1]{0,1:T(1,128)S(1)}, pred[8,8]{1,0:T(8,128)(4,1)S(1)}, /*index...) while((s32[]{:T(128)}, f32[512,1]{0,1:T(1,128)S(1)}, ...), condition=%wide.region_10.10_spmd, body=%wide.region_4.9_spmd.sunk | while | flops 136316448 | bytes 4764170 | solution.py:105
  339.4 51.8 %while.56 = (s32[]{:T(128)}, f32[512,128]{1,0:T(8,128)S(1)}, f32[4096,128]{1,0:T(8,128)}, f32[4096,128]{1,0:T(8,128)}, pred[8,8]{1,0:T(8,128)(4,1)S(1)}, /*index...) while((s32[]{:T(128)}, f32[512,128]{1,0:T(8,128)S(1)}, ...), condition=%wide.region_14.14_spmd, body=%wide.region_11.13_spmd.sunk | while | flops 337969184 | bytes 7221814 | solution.py:136
  340.7 5.2 conditional.5
  347.2 5.2 conditional.5
  353.6 5.2 conditional.5
  360.1 5.2 conditional.5
  366.6 5.2 conditional.5
  373.1 5.2 conditional.5
  379.6 5.2 conditional.5
  386.0 5.2 conditional.5
  398.8 6.5 fusion.48
  405.7 59.3 %copy.60 = bf16[1,1,1,4096,384]{4,2,1,0,3:T(2,128)(2,1)} copy(bf16[1,1,1,4096,384]{4,3,2,1,0:T(8,128)(2,1)S(1)} %pad_maximum_fusion) | data formatting | bytes 6291456 | tf_op jit(solution)/shard_map/concatenate | solution.py:154
  465.6 68.9 %reduce = bf16[4096,384]{1,0:T(8,128)(2,1)} reduce(bf16[4096,1,1,1,384]{4,3,2,1,0:T(2,128)(2,1)} %bitcast.124, bf16[]{:T(256)} %broadcast.299), dimensions={1,2,3}, to_apply=%bitcast.119.reduce_sub_computation | reduce | bytes 6291458
  534.4 7.6 reshape.285
  542.0 298.3 %all-to-all-start.1 = ((bf16[32,2,24576]{2,1,0:T(2,128)(2,1)}), bf16[32,2,24576]{2,1,0:T(2,128)(2,1)}, u32[]{:S(2)}, u32[]{:S(2)}) async-start(bf16[32,2,24576]{2,1,0:T(2,128)(2,1)} %reshape.285), calls=%async_computation.1 | async-start | bytes 6291456 | tf_op jit(solution)/shard_map/all_to_all | solution.py:188
  840.3 108.5 %psum.7 = f32[2,128]{1,0:T(2,128)S(1)} all-reduce(f32[2,128]{1,0:T(2,128)S(1)} %pad_maximum_fusion.1), channel_id=1, replica_groups=mesh['dp'=8,'ulysses'=32] {'dp','ulysses'}, use_global_device_ids=true, to_apply=%region_20.21 | all-reduce | flops 256 | bytes 2048 | tf_op jit(solution)/shard_map/psum | solution.py:203
  949.4 18.9 %reshape.286 = bf16[4096,1,1,1,384]{4,3,2,1,0:T(2,128)(2,1)} reshape(bf16[32,2,24576]{2,1,0:T(2,128)(2,1)} %all-to-all-done.1) | data formatting | bytes 6291456
  (727 shorter events, 350.9 us)
Async XLA Ops:
  0.6 35.6 %copy-start = (s32[24,32,32]{2,1,0:T(8,128)S(1)}, s32[24,32,32]{2,1,0:T(8,128)}, u32[]{:S(2)}) copy-start(s32[24,32,32]{2,1,0:T(8,128)} %param.23) | copy-start | bytes 294916
  25.1 58.9 %all-to-all-start = ((bf16[32,1,1,128,512]{4,3,2,1,0:T(8,128)(2,1)}), bf16[32,1,1,128,512]{4,3,2,1,0:T(8,128)(2,1)}, u32[]{:S(2)}, u32[]{:S(2)}) async-start(bf16[32,1,1,128,512]{4,3,2,1,0:T(8,128)(2,1)} %fusion.24), calls=%async_computation | async-start | bytes 8388608 | tf_op jit(solution)/shard_map/all_to_all | solution.py:179
  86.7 2.7 copy-start.5
  86.7 2.7 copy-start.6
  392.0 2.2 copy-start.2
  394.2 4.6 copy-start.3
  542.0 407.4 %all-to-all-start.1 = ((bf16[32,2,24576]{2,1,0:T(2,128)(2,1)}), bf16[32,2,24576]{2,1,0:T(2,128)(2,1)}, u32[]{:S(2)}, u32[]{:S(2)}) async-start(bf16[32,2,24576]{2,1,0:T(2,128)(2,1)} %reshape.285), calls=%async_computation.1 | async-start | bytes 6291456 | tf_op jit(solution)/shard_map/all_to_all | solution.py:188
  975.2 2.3 copy-start.4
  975.2 4.7 copy-start.1
where the time goes:
time: 987 us; the launch traced here: 980 us
  starting transfers between devices  307 us (31%)
  matrix products  181 us (18%)
  local copies, waits for them, and re-layouts  174 us (18%)
  other arithmetic  111 us (11%)
  blocking collectives  109 us (11%)
  loops' own time  48.6 us (5%)
  waiting for transfers between devices  45.4 us (5%)
    all_to_all x1, starting transfers between devices, body(): lax.all_to_all(backward.astype(jnp.bfloat16), 'ulysses', split_axis=3, co...  298 us
    dot_general x64, matrix products, dot_cols(): lax.dot_general(left_side, right_side, (((0,), (0,)), ((), ())), preferre...  125 us
    psum x1, blocking collectives, body(): summed = lax.psum(gain_part, ('dp', 'ulysses'))  109 us
    unnamed x1, other arithmetic  68.9 us
    concatenate x1, local copies, waits for them, and re-layouts, item_grads(): return (jnp.concatenate([grad_q, grad_k, grad_v], axis=1), gain_part)  59.3 us
    all_to_all x1, waiting for transfers between devices, body(): lax.all_to_all(outgoing, 'ulysses', split_axis=0, concat_axis=3, tiled=True)  45.4 us
    dot_general x128, matrix products, dot_rows(): lax.dot_general(left_side, right_side, (((1,), (1,)), ((), ())), preferre...  42.4 us
    unnamed x22, local copies, waits for them, and re-layouts  38.3 us
  transfers between devices with their start and end apart: 2, of which 1 were waited for; matrix products, arithmetic and copies ran while one was open for 0% of the time, Pallas kernels for 0%

commit v1 on v0

v1 whole, which is shorter than its diff:
```python
import functools

import jax
import jax.numpy as jnp
from jax import lax
from jax.experimental import pallas as pl
from jax.experimental.pallas import tpu as pltpu
from jax.sharding import PartitionSpec as P

HEADS = 24
HEAD_DIM = 128
SPLITS = 8
BLOCK = 128
ITEMS = 32
GROUP = 8

NORM_EPS = 1e-06
NEG_FILL = -1e30
SCALE = HEAD_DIM ** (-0.5)
LOG2E = 1.4426950408889634
SCORE2 = SCALE * LOG2E
SAFE_BOUND = 80.0
F32 = jnp.float32
BF16 = jnp.bfloat16


def pack_kernel(heads_ref, q_ref, k_ref, v_ref, o_ref, out_ref):
    def move(slot, carry):
        at = pl.multiple_of(heads_ref[slot] * HEAD_DIM, HEAD_DIM)
        for which, src in enumerate((q_ref, k_ref, v_ref, o_ref)):
            out_ref[slot, which] = src[:, pl.ds(at, HEAD_DIM)]
        return carry

    lax.fori_loop(0, ITEMS, move, 0)


def pack(item_heads, q_raw, k_raw, values, grad_out):
    rows = q_raw.shape[0]
    vmem = pl.BlockSpec(memory_space=pltpu.VMEM)
    return pl.pallas_call(
        pack_kernel,
        out_shape=jax.ShapeDtypeStruct((ITEMS, 4, rows, HEAD_DIM), BF16),
        in_specs=[pl.BlockSpec(memory_space=pltpu.SMEM)] + [vmem] * 4,
        out_specs=vmem,
        compiler_params=pltpu.CompilerParams(vmem_limit_bytes=24 * 2**20),
        name="pack_heads",
    )(item_heads, q_raw, k_raw, values, grad_out)


def inv_spread(raw_float):
    return lax.rsqrt(jnp.mean(raw_float * raw_float, axis=-1, keepdims=True) + NORM_EPS)


def norm_back(raw_float, gain, grad_normed):
    inv = inv_spread(raw_float)
    unit = raw_float * inv
    scaled = gain * grad_normed
    inner = jnp.sum(scaled * unit, axis=-1, keepdims=True) * (1.0 / HEAD_DIM)
    return (scaled - unit * inner) * inv, grad_normed * unit


def fold_rows(full):
    return jnp.sum(full.reshape(-1, 8, full.shape[-1]), axis=0)


def item_kernel(
    nb, info_ref, list_ref, gain_ref, in_ref, out_ref, part_ref,
    kv, kt, probs, dprobs, acc, left, right, sums,
):
    first, last, careful = info_ref[0], info_ref[1], info_ref[2]
    q_gain = gain_ref[0:1, :]
    k_gain = gain_ref[1:2, :]
    slots = list_ref.shape[0] // nb

    def prepare(j, carry):
        raw = in_ref[j, 1].astype(F32)
        normed = (raw * inv_spread(raw) * k_gain).astype(BF16)
        kv[j, :, :HEAD_DIM] = normed
        kv[j, :, HEAD_DIM:] = in_ref[j, 2]
        kt[j] = normed.T
        acc[j] = jnp.zeros((BLOCK, 2 * HEAD_DIM), F32)
        out_ref[j, 0] = jnp.zeros((BLOCK, HEAD_DIM), BF16)
        return carry

    lax.fori_loop(0, nb, prepare, 0)
    kv[nb] = jnp.zeros((BLOCK, 2 * HEAD_DIM), BF16)
    kt[nb] = jnp.zeros((HEAD_DIM, BLOCK), BF16)
    acc[nb] = jnp.zeros((BLOCK, 2 * HEAD_DIM), F32)
    left[...] = jnp.zeros((2 * HEAD_DIM, 2 * BLOCK), BF16)
    right[...] = jnp.zeros((2 * BLOCK, 2 * HEAD_DIM), BF16)
    part_ref[...] = jnp.zeros((16, HEAD_DIM), F32)

    def query_block(i, carry):
        raw = in_ref[i, 0].astype(F32)
        normed = (raw * inv_spread(raw) * q_gain).astype(BF16)
        o_block = in_ref[i, 3]
        left[:HEAD_DIM, :BLOCK] = normed.T
        left[HEAD_DIM:, BLOCK:] = o_block.T
        right[:BLOCK, :HEAD_DIM] = o_block
        right[BLOCK:, HEAD_DIM:] = normed
        base = i * slots
        count = info_ref[8 + i]
        groups = (count + (GROUP - 1)) // GROUP

        def bias_of(at):
            return jnp.where(at < count, 0.0, NEG_FILL)

        sums[0:1, :] = jnp.zeros((1, BLOCK), F32)

        @pl.when(careful > 0)
        def _():
            def peak_step(at, peak):
                j = list_ref[base + at]
                scores = jnp.dot(kv[j, :, :HEAD_DIM], left[:HEAD_DIM, :BLOCK], preferred_element_type=F32)
                return jnp.maximum(peak, jnp.max(scores.reshape(-1, 8, BLOCK), axis=0))

            peak = lax.fori_loop(0, count, peak_step, jnp.full((8, BLOCK), NEG_FILL, F32))
            sums[0:1, :] = jnp.max(peak, axis=0, keepdims=True) * SCORE2

        shift = sums[0:1, :]

        def score_step(g, stats):
            total, dotted = stats
            at = g * GROUP
            js = [list_ref[base + at + u] for u in range(GROUP)]
            for u in range(GROUP):
                both = jnp.dot(kv[js[u]], left[...], preferred_element_type=F32)
                weights = jnp.exp2(both[:, :BLOCK] * SCORE2 + (bias_of(at + u) - shift))
                grads = both[:, BLOCK:]
                probs[at + u] = weights
                dprobs[at + u] = grads
                total = total + fold_rows(weights)
                dotted = dotted + fold_rows(weights * grads)
            return total, dotted

        zero = jnp.zeros((8, BLOCK), F32)
        total, dotted = lax.fori_loop(0, groups, score_step, (zero, zero))
        inv_total = 1.0 / jnp.sum(total, axis=0, keepdims=True)
        row_delta = jnp.sum(dotted, axis=0, keepdims=True) * inv_total

        def grad_step(g, grad_qt):
            at = g * GROUP
            js = [list_ref[base + at + u] for u in range(GROUP)]
            s_parts = []
            for u in range(GROUP):
                weights = probs[at + u] * inv_total
                scores = (weights * (dprobs[at + u] - row_delta)).astype(BF16)
                s_parts.append(scores)
                acc[js[u]] += jnp.dot(
                    jnp.concatenate([weights.astype(BF16), scores], axis=1), right[...], preferred_element_type=F32
                )
            scores_half = jnp.concatenate(s_parts, axis=0)
            keys_t = jnp.concatenate([kt[j] for j in js], axis=1)
            return grad_qt + jnp.dot(keys_t, scores_half, preferred_element_type=F32)

        grad_qt = lax.fori_loop(0, groups, grad_step, jnp.zeros((HEAD_DIM, BLOCK), F32))
        grad, gains = norm_back(raw, q_gain, grad_qt.T * SCALE)
        out_ref[i, 0] = grad.astype(BF16)
        part_ref[0:8, :] += fold_rows(gains)
        return carry

    lax.fori_loop(first, last, query_block, 0)

    def finish(j, carry):
        grad, gains = norm_back(in_ref[j, 1].astype(F32), k_gain, acc[j, :, HEAD_DIM:] * SCALE)
        out_ref[j, 1] = grad.astype(BF16)
        out_ref[j, 2] = acc[j, :, :HEAD_DIM].astype(BF16)
        part_ref[8:16, :] += fold_rows(gains)
        return carry

    lax.fori_loop(0, nb, finish, 0)


def item_grads(info, block_list, gains, arrived):
    nb = arrived.shape[0]
    slots = block_list.shape[0] // nb
    smem = pl.BlockSpec(memory_space=pltpu.SMEM)
    vmem = pl.BlockSpec(memory_space=pltpu.VMEM)
    return pl.pallas_call(
        functools.partial(item_kernel, nb),
        out_shape=(
            jax.ShapeDtypeStruct((nb, 3, BLOCK, HEAD_DIM), BF16),
            jax.ShapeDtypeStruct((16, HEAD_DIM), F32),
        ),
        in_specs=[smem, smem, vmem, vmem],
        out_specs=(vmem, vmem),
        scratch_shapes=[
            pltpu.VMEM((nb + 1, BLOCK, 2 * HEAD_DIM), BF16),
            pltpu.VMEM((nb + 1, HEAD_DIM, BLOCK), BF16),
            pltpu.VMEM((slots, BLOCK, BLOCK), F32),
            pltpu.VMEM((slots, BLOCK, BLOCK), F32),
            pltpu.VMEM((nb + 1, BLOCK, 2 * HEAD_DIM), F32),
            pltpu.VMEM((2 * HEAD_DIM, 2 * BLOCK), BF16),
            pltpu.VMEM((2 * BLOCK, 2 * HEAD_DIM), BF16),
            pltpu.VMEM((8, BLOCK), F32),
        ],
        compiler_params=pltpu.CompilerParams(vmem_limit_bytes=40 * 2**20),
        name="item_grads",
    )(info, block_list, gains, arrived)


def merge_kernel(heads_ref, in_ref, q_ref, k_ref, v_ref):
    outs = (q_ref, k_ref, v_ref)

    def pair(p, carry):
        at = pl.multiple_of(heads_ref[2 * p] * HEAD_DIM, HEAD_DIM)
        for which, out in enumerate(outs):
            both = in_ref[2 * p, which].astype(F32) + in_ref[2 * p + 1, which].astype(F32)
            out[:, pl.ds(at, HEAD_DIM)] = both.astype(BF16)
        return carry

    def single(slot, carry):
        at = pl.multiple_of(heads_ref[slot] * HEAD_DIM, HEAD_DIM)
        for which, out in enumerate(outs):
            out[:, pl.ds(at, HEAD_DIM)] = in_ref[slot, which]
        return carry

    lax.fori_loop(0, SPLITS, pair, 0)
    lax.fori_loop(2 * SPLITS, ITEMS, single, 0)


def merge(item_heads, returned):
    rows = returned.shape[2]
    vmem = pl.BlockSpec(memory_space=pltpu.VMEM)
    wide = jax.ShapeDtypeStruct((rows, HEADS * HEAD_DIM), BF16)
    return pl.pallas_call(
        merge_kernel,
        out_shape=(wide, wide, wide),
        in_specs=[pl.BlockSpec(memory_space=pltpu.SMEM), vmem],
        out_specs=(vmem, vmem, vmem),
        compiler_params=pltpu.CompilerParams(vmem_limit_bytes=24 * 2**20),
        name="merge_heads",
    )(item_heads, returned)


def plan_items(block_masks):
    totals = jnp.sum((block_masks > 0).astype(jnp.int32), axis=(1, 2))
    heads = jnp.arange(HEADS, dtype=jnp.int32)
    ahead = (totals[None, :] > totals[:, None]) | (
        (totals[None, :] == totals[:, None]) & (heads[None, :] < heads[:, None])
    )
    rank = jnp.sum(ahead.astype(jnp.int32), axis=1)
    counter = jnp.arange(ITEMS, dtype=jnp.int32)
    wanted = jnp.where(counter < 2 * SPLITS, counter // 2, counter - SPLITS)
    return jnp.sum(jnp.where(rank[None, :] == wanted[:, None], heads[None, :], 0), axis=1)


def block_lists(mask_head):
    nb = mask_head.shape[0]
    on = (mask_head > 0).astype(jnp.int32)
    lower = (jnp.arange(nb)[:, None] < jnp.arange(nb)[None, :]).astype(jnp.int32)
    place = jnp.sum(on[:, :, None] * lower[None, :, :], axis=1)
    slot = jnp.arange(nb + GROUP, dtype=jnp.int32)
    hit = (on[:, :, None] > 0) & (place[:, :, None] == slot[None, None, :])
    which = jnp.arange(nb, dtype=jnp.int32)[None, :, None]
    counts = jnp.sum(on, axis=1)
    lists = nb + jnp.sum(jnp.where(hit, which - nb, 0), axis=1)
    return counts, lists


def body(q_raw, k_raw, values, grad_out, q_gain, k_gain, block_masks):
    device_rank = lax.axis_index("ulysses")
    tok_rows, width = q_raw.shape[1:]
    nb = block_masks.shape[1]
    seq_len = tok_rows * lax.axis_size("ulysses")
    videos = lax.axis_size("dp")
    item_heads = plan_items(block_masks)
    outgoing = pack(item_heads, q_raw[0], k_raw[0], values[0], grad_out[0])
    arrived = lax.all_to_all(outgoing, "ulysses", split_axis=0, concat_axis=0, tiled=True)
    head = lax.dynamic_index_in_dim(item_heads, device_rank, 0, keepdims=False)
    counts, lists = block_lists(lax.dynamic_index_in_dim(block_masks, head, 0, keepdims=False))
    split = device_rank < 2 * SPLITS
    half = device_rank % 2
    first = jnp.where(split, half * (nb // 2), 0)
    last = jnp.where(split, (half + 1) * (nb // 2), nb)
    bound = 1.02 * HEAD_DIM * SCORE2 * jnp.max(jnp.abs(q_gain)) * jnp.max(jnp.abs(k_gain))
    careful = jnp.where(bound < SAFE_BOUND, 0, 1)
    info = jnp.concatenate(
        [jnp.stack([first, last, careful]).astype(jnp.int32), jnp.zeros((5,), jnp.int32), counts]
    )
    gains = jnp.stack([q_gain, k_gain])
    grads, part = item_grads(info, lists.reshape(-1), gains, arrived)
    returned = lax.all_to_all(grads, "ulysses", split_axis=0, concat_axis=0, tiled=True)
    summed = lax.psum(jnp.sum(part.reshape(2, 8, HEAD_DIM), axis=1), ("dp", "ulysses"))
    grad_q, grad_k, grad_v = merge(item_heads, returned)
    gain_grads = summed * (videos * seq_len * HEADS) ** (-0.5)
    return (grad_q[None], grad_k[None], grad_v[None], gain_grads)


def solution(mesh):
    tokens = P("dp", "ulysses", None)
    return jax.shard_map(
        body,
        mesh=mesh,
        in_specs=(tokens, tokens, tokens, tokens, P(), P(), P()),
        out_specs=(tokens, tokens, tokens, P()),
        check_vma=False,
    )
```

time: 987 us -> 313 us (0.32)
  starting transfers between devices: 307 us -> 12.6 us
  matrix products: 181 us -> 0 us
  local copies, waits for them, and re-layouts: 174 us -> 8.91 us
  Pallas kernels: 0 us -> 130 us
  other arithmetic: 111 us -> 5.04 us
  loops' own time: 48.6 us -> 0 us
    all_to_all x2, starting transfers between devices: 307 us -> 12.6 us  [the longest x1 8.78 us: body(): lax.all_to_all(outgoing, 'ulysses', split_axis=0, concat_axis=0, tiled=True)]
    dot_general x225 -> x0, matrix products: 181 us -> none  [the longest x64 125 us: dot_cols(): lax.dot_general(left_side, right_side, (((0,), (0,)), ((), ())), preferre...]
    pallas_call x0 -> x3, Pallas kernels: none -> 130 us  [the longest x1 126 us: item_grads(): pl.pallas_call(functools.partial(item_kernel, nb), out_shape=(jax.ShapeDt...]
    unnamed x1 -> x0, other arithmetic: 68.9 us -> none
    concatenate x1, local copies, waits for them, and re-layouts: 59.3 us -> 0.08 us  [body(): jnp.concatenate([jnp.stack([first, last, careful]).astype(jnp.int32), jnp...]
    another operation x73 -> x0, loops' own time: 48.6 us -> none  [the longest x4 22.6 us: query_tile(): run_max, run_sum, run_dot = lax.fori_loop(0, tile_count, stats_step, start)]
    dynamic_slice x72 -> x1, local copies, waits for them, and re-layouts: 45.2 us -> 0.59 us  [body(): head = lax.dynamic_index_in_dim(item_heads, device_rank, 0, keepdims=False)]
    unnamed x22 -> x16, local copies, waits for them, and re-layouts: 38.3 us -> 8.16 us
  transfers between devices with their start and end apart: 2 -> 2, of which waited for: 1 -> 1; matrix products, arithmetic and copies ran while one was open for 0% -> 1% of each run, Pallas kernels for 0% -> 0%
where the time goes in v1:
time: 313 us; the launch traced here: 312 us
  Pallas kernels  130 us (42%)
  blocking collectives  107 us (34%)
  waiting for transfers between devices  43.5 us (14%)
  starting transfers between devices  12.6 us (4%)
  local copies, waits for them, and re-layouts  8.91 us (3%)
  other arithmetic  5.04 us (2%)
  between operations  4.06 us (1%)
    pallas_call x1, Pallas kernels, item_grads(): pl.pallas_call(functools.partial(item_kernel, nb), out_shape=(jax.ShapeDt...  126 us
    psum x1, blocking collectives, body(): lax.psum(jnp.sum(part.reshape(2, 8, HEAD_DIM), axis=1), ('dp', 'ulysses'))  107 us
    all_to_all x1, waiting for transfers between devices, body(): lax.all_to_all(outgoing, 'ulysses', split_axis=0, concat_axis=0, tiled=True)  43.5 us
    all_to_all x1, starting transfers between devices, body(): lax.all_to_all(outgoing, 'ulysses', split_axis=0, concat_axis=0, tiled=True)  8.78 us
    unnamed x16, local copies, waits for them, and re-layouts  8.16 us
  transfers between devices with their start and end apart: 2, of which 1 were waited for; matrix products, arithmetic and copies ran while one was open for 1% of the time, Pallas kernels for 0%

profile of v1, /device:TPU:1, one launch (start us, length us, event | category | flops | bytes accessed | tf_op | source)
XLA Modules:
  0.0 311.9 jit_solution(5681080173653648293)
XLA Ops:
  0.6 1.5 convert_reduce_fusion
  2.2 0.2 convert_reduce_fusion.2
  2.4 0.1 select_reduce_fusion.1.heads_ref
  2.5 0.0 copy-start.2
  2.5 1.1 copy-done.2
  3.6 0.0 copy-start.3
  3.6 1.1 copy-done.3
  4.7 0.0 copy-start.4
  4.7 1.1 copy-done.4
  5.9 0.0 copy-start.5
  5.9 1.1 copy-done.5
  7.0 1.8 pack_heads.1
  8.8 0.0 copy-start
  8.8 2.0 copy-done
  10.8 0.0 copy-start.6
  10.8 0.0 copy-start.7
  10.8 8.8 %all-to-all-start = ((bf16[32,4,128,128]{3,2,1,0:T(8,128)(2,1)}), bf16[32,4,128,128]{3,2,1,0:T(8,128)(2,1)}, u32[]{:S(2)}, u32[]{:S(2)}) async-start(bf16[32,4,128,128]{3,2,1,0:T(8,128)(2,1)} %copy-done), calls=%async_computation | async-start | bytes 8388608 | tf_op jit(solution)/shard_map/all_to_all | solution.py:269
  19.6 0.6 dynamic_slice.8
  22.1 0.7 broadcast_compare_fusion
  22.9 0.2 multiply_reduce_fusion
  23.1 0.4 select_reduce_fusion
  23.5 0.1 add.49.list_ref
  23.6 0.0 copy-done.6
  23.6 0.6 abs_reduce_fusion.1
  24.8 0.0 copy-done.7
  24.8 0.6 abs_reduce_fusion
  26.1 0.1 convert_reduce_fusion.1
  26.2 0.1 concatenate.3.info_ref
  26.3 43.5 %all-to-all-done.in_ref = bf16[32,4,128,128]{3,2,1,0:T(8,128)(2,1)} async-done(((bf16[32,4,128,128]{3,2,1,0:T(8,128)(2,1)}), bf16[32,4,128,128]{3,2,1,0:T(8,128)(2,1)}, u32[]{:S(2)}, u32[]{:S(2)}) %all-to-all-start) | async-done | bytes 4194336 | tf_op jit(solution)/shard_map/all_to_all | solution.py:269
  69.8 125.8 %item_grads.1 = (bf16[32,3,128,128]{3,2,1,0:T(8,128)(2,1)S(1)}, f32[16,128]{1,0:T(8,128)S(1)}) custom-call(s32[40]{0:T(128)S(1)} %concatenate.3.info_ref, s32[1280]{0:T(1024)S(1)} %add.49.list_ref, f32[2,128]{1,0:T(2,128)S(1)} %pad_maximum_fusion.gain_ref, bf16[32,4,128,128]{3,2,1,0:T(8,128)(2,1)} %all-to-all-done.in_ref), custom_call_target="tpu_custom_call" | custom-call | tf_op jit(solution)/shard_map/item_grads/pallas_call | solution.py:179
  195.7 0.0 copy-start.1
  195.7 1.7 copy-done.1
  197.3 3.9 %all-to-all-start.1 = ((bf16[32,3,128,128]{3,2,1,0:T(8,128)(2,1)}), bf16[32,3,128,128]{3,2,1,0:T(8,128)(2,1)S(1)}, u32[]{:S(2)}, u32[]{:S(2)}) async-start(bf16[32,3,128,128]{3,2,1,0:T(8,128)(2,1)} %copy-done.1), calls=%async_computation.1 | async-start | bytes 6291456 | tf_op jit(solution)/shard_map/all_to_all | solution.py:283
  201.2 107.4 %psum.7 = f32[2,128]{1,0:T(2,128)S(1)} all-reduce(f32[2,128]{1,0:T(2,128)S(1)} %bitcast_reduce_fusion), channel_id=1, replica_groups=mesh['dp'=8,'ulysses'=32] {'dp','ulysses'}, use_global_device_ids=true, to_apply=%region_9.10 | all-reduce | flops 256 | bytes 2048 | tf_op jit(solution)/shard_map/psum | solution.py:284
  308.6 0.6 broadcast_multiply_fusion
  309.2 0.0 all-to-all-done.1.in_ref
  309.2 2.7 merge_heads.1
  (8 shorter events, 0.0 us)
Async XLA Ops:
  2.5 1.1 copy-start.2
  3.6 1.1 copy-start.3
  4.7 1.1 copy-start.4
  5.9 1.1 copy-start.5
  8.8 2.0 copy-start
  10.8 12.8 %copy-start.6 = (f32[128]{0:T(128)S(1)}, f32[128]{0:T(128)}, u32[]{:S(2)}) copy-start(f32[128]{0:T(128)} %param.11) | copy-start | bytes 1540
  10.8 14.1 %copy-start.7 = (f32[128]{0:T(128)S(1)}, f32[128]{0:T(128)}, u32[]{:S(2)}) copy-start(f32[128]{0:T(128)} %param.12) | copy-start | bytes 1540
  10.8 59.0 %all-to-all-start = ((bf16[32,4,128,128]{3,2,1,0:T(8,128)(2,1)}), bf16[32,4,128,128]{3,2,1,0:T(8,128)(2,1)}, u32[]{:S(2)}, u32[]{:S(2)}) async-start(bf16[32,4,128,128]{3,2,1,0:T(8,128)(2,1)} %copy-done), calls=%async_computation | async-start | bytes 8388608 | tf_op jit(solution)/shard_map/all_to_all | solution.py:269
  195.7 1.7 copy-start.1
  197.3 111.8 %all-to-all-start.1 = ((bf16[32,3,128,128]{3,2,1,0:T(8,128)(2,1)}), bf16[32,3,128,128]{3,2,1,0:T(8,128)(2,1)S(1)}, u32[]{:S(2)}, u32[]{:S(2)}) async-start(bf16[32,3,128,128]{3,2,1,0:T(8,128)(2,1)} %copy-done.1), calls=%async_computation.1 | async-start | bytes 6291456 | tf_op jit(solution)/shard_map/all_to_all | solution.py:283

commit v2 on v1

v2 whole, which is shorter than its diff:
```python
import functools

import jax
import jax.numpy as jnp
from jax import lax
from jax.experimental import pallas as pl
from jax.experimental.pallas import tpu as pltpu
from jax.sharding import PartitionSpec as P

HEADS = 24
HEAD_DIM = 128
SPLITS = 8
BLOCK = 128
ITEMS = 32
DENSE_GROUP = 16
SPARSE_GROUP = 4
DENSE_FROM = 12
CHUNK = 4
UNROLL = 4

NORM_EPS = 1e-06
NEG_FILL = -1e30
SCALE = HEAD_DIM ** (-0.5)
LOG2E = 1.4426950408889634
SCORE2 = SCALE * LOG2E
SAFE_BOUND = 50.0
F32 = jnp.float32
BF16 = jnp.bfloat16


def pack_kernel(heads_ref, q_ref, k_ref, v_ref, o_ref, out_ref, wide, tall, in_sems, out_sems):
    rows = q_ref.shape[0]
    part = rows // CHUNK
    loads, stores = [], []
    for which, src in enumerate((q_ref, k_ref, v_ref, o_ref)):
        for c in range(CHUNK):
            at = pl.ds(c * part, part)
            copy = pltpu.make_async_copy(src.at[at], wide.at[which, at], in_sems.at[which, c])
            copy.start()
            loads.append(copy)
    for which in range(4):
        for c in range(CHUNK):
            loads[which * CHUNK + c].wait()

        def move(slot, carry, which=which):
            at = pl.multiple_of(heads_ref[slot] * HEAD_DIM, HEAD_DIM)
            tall[which, slot] = wide[which, :, pl.ds(at, HEAD_DIM)]
            return carry

        lax.fori_loop(0, ITEMS, move, 0)
        copy = pltpu.make_async_copy(tall.at[which], out_ref.at[:, which], out_sems.at[which])
        copy.start()
        stores.append(copy)
    for copy in stores:
        copy.wait()


def pack(item_heads, q_raw, k_raw, values, grad_out):
    rows, width = q_raw.shape
    hbm = pl.BlockSpec(memory_space=pltpu.HBM)
    return pl.pallas_call(
        pack_kernel,
        out_shape=jax.ShapeDtypeStruct((ITEMS, 4, rows, HEAD_DIM), BF16),
        in_specs=[pl.BlockSpec(memory_space=pltpu.SMEM)] + [hbm] * 4,
        out_specs=hbm,
        scratch_shapes=[
            pltpu.VMEM((4, rows, width), BF16),
            pltpu.VMEM((4, ITEMS, rows, HEAD_DIM), BF16),
            pltpu.SemaphoreType.DMA((4, CHUNK)),
            pltpu.SemaphoreType.DMA((4,)),
        ],
        compiler_params=pltpu.CompilerParams(vmem_limit_bytes=60 * 2**20),
        name="pack_heads",
    )(item_heads, q_raw, k_raw, values, grad_out)


def inv_spread(raw_float):
    return lax.rsqrt(jnp.mean(raw_float * raw_float, axis=-1, keepdims=True) + NORM_EPS)


def norm_back(raw_float, gain, grad_normed):
    inv = inv_spread(raw_float)
    unit = raw_float * inv
    scaled = gain * grad_normed
    inner = jnp.sum(scaled * unit, axis=-1, keepdims=True) * (1.0 / HEAD_DIM)
    return (scaled - unit * inner) * inv, grad_normed * unit


def fold_rows(full):
    return jnp.sum(full.reshape(-1, 8, full.shape[-1]), axis=0)


def item_kernel(
    nb, info_ref, list_ref, gain_ref, hbm_ref, qk_ref, v_ref, part_ref,
    in_ref, qk_out, v_out, in_sems, qk_sems, v_sems, kv, kt, pairs_even, pairs_odd, acc, left, right, grad_qt, shifts,
):
    first, last, careful = info_ref[0], info_ref[1], info_ref[2]
    q_gain = gain_ref[0:1, :]
    k_gain = gain_ref[1:2, :]
    slots = list_ref.shape[0] // nb
    zero_half = jnp.zeros((BLOCK, HEAD_DIM), BF16)

    def load(step):
        at = pl.ds(step * UNROLL, UNROLL)
        return pltpu.make_async_copy(hbm_ref.at[at], in_ref.at[at], in_sems.at[step])

    def store(step):
        at = pl.ds(step * UNROLL, UNROLL)
        return (
            pltpu.make_async_copy(qk_out.at[at], qk_ref.at[at], qk_sems.at[step]),
            pltpu.make_async_copy(v_out.at[at], v_ref.at[at], v_sems.at[step]),
        )

    for step in range(nb // UNROLL):
        load(step).start()

    def prepare_keys(step, carry):
        load(step).wait()
        for u in range(UNROLL):
            j = step * UNROLL + u
            raw = in_ref[j, 1].astype(F32)
            normed = (raw * inv_spread(raw) * k_gain).astype(BF16)
            kv[j, :, :HEAD_DIM] = normed
            kv[j, :, HEAD_DIM:] = in_ref[j, 2]
            kt[j] = normed.T
            acc[j] = jnp.zeros((BLOCK, 2 * HEAD_DIM), F32)
            qk_out[j, 0] = zero_half
        return carry

    def prepare_queries(step, carry):
        for u in range(UNROLL):
            i = first + step * UNROLL + u
            raw = in_ref[i, 0].astype(F32)
            normed = (raw * inv_spread(raw) * q_gain).astype(BF16)
            o_block = in_ref[i, 3]
            left[i, :HEAD_DIM, :BLOCK] = normed.T
            left[i, HEAD_DIM:, BLOCK:] = o_block.T
            left[i, :HEAD_DIM, BLOCK:] = zero_half
            left[i, HEAD_DIM:, :BLOCK] = zero_half
            right[i, :BLOCK, :HEAD_DIM] = o_block
            right[i, BLOCK:, HEAD_DIM:] = normed
            right[i, :BLOCK, HEAD_DIM:] = zero_half
            right[i, BLOCK:, :HEAD_DIM] = zero_half
            shifts[i] = jnp.zeros((8, BLOCK), F32)
        return carry

    lax.fori_loop(0, nb // UNROLL, prepare_keys, 0)
    lax.fori_loop(0, (last - first) // UNROLL, prepare_queries, 0)
    kv[nb] = jnp.zeros((BLOCK, 2 * HEAD_DIM), BF16)
    kt[nb] = zero_half
    acc[nb] = jnp.zeros((BLOCK, 2 * HEAD_DIM), F32)

    def clear(at, carry):
        pairs_even[at] = jnp.zeros((BLOCK, 2 * BLOCK), F32)
        pairs_odd[at] = jnp.zeros((BLOCK, 2 * BLOCK), F32)
        return carry

    lax.fori_loop(0, slots, clear, 0)
    part_ref[...] = jnp.zeros((16, HEAD_DIM), F32)

    @pl.when(careful > 0)
    def _():
        def peak_row(i, carry):
            def peak_step(at, peak):
                j = list_ref[i * slots + at]
                scores = jnp.dot(kv[j, :, :HEAD_DIM], left[i, :HEAD_DIM, :BLOCK], preferred_element_type=F32)
                return jnp.maximum(peak, jnp.max(scores.reshape(-1, 8, BLOCK), axis=0))

            peak = lax.fori_loop(0, info_ref[8 + i], peak_step, jnp.full((8, BLOCK), NEG_FILL, F32))
            shifts[i] = jnp.broadcast_to(jnp.max(peak, axis=0, keepdims=True) * SCORE2, (8, BLOCK))
            return carry

        lax.fori_loop(first, last, peak_row, 0)

    def groups_of(i, size):
        return (info_ref[8 + i] + (size - 1)) // size

    def score_group(size, pairs, i, g, stats):
        total, dotted = stats
        count = info_ref[8 + i]
        shift = shifts[i, 0:1, :]
        for u in range(size):
            at = g * size + u
            both = jnp.dot(kv[list_ref[i * slots + at]], left[i], preferred_element_type=F32)
            weights = jnp.exp2(both[:, :BLOCK] * SCORE2 + (jnp.where(at < count, 0.0, NEG_FILL) - shift))
            grads = both[:, BLOCK:]
            pairs[at, :, :BLOCK] = weights
            pairs[at, :, BLOCK:] = grads
            total = total + fold_rows(weights)
            dotted = dotted + fold_rows(weights * grads)
        return total, dotted

    def grad_group(size, pairs, i, g, inv_total, row_delta, total_qt):
        halves, keys = [], []
        for u in range(size):
            at = g * size + u
            j = list_ref[i * slots + at]
            weights = pairs[at, :, :BLOCK] * inv_total
            half = (weights * (pairs[at, :, BLOCK:] - row_delta)).astype(BF16)
            acc[j] += jnp.dot(
                jnp.concatenate([weights.astype(BF16), half], axis=1), right[i], preferred_element_type=F32
            )
            halves.append(half)
            keys.append(kt[j])
        return total_qt + jnp.dot(
            jnp.concatenate(keys, axis=1), jnp.concatenate(halves, axis=0), preferred_element_type=F32
        )

    zero = jnp.zeros((8, BLOCK), F32)
    def attend(size):
        stats = lax.fori_loop(
            0, groups_of(first, size), lambda g, s: score_group(size, pairs_even, first, g, s), (zero, zero)
        )

        def query_block(i, later, mine, other, stats):
            total, dotted = stats
            inv_total = 1.0 / jnp.sum(total, axis=0, keepdims=True)
            row_delta = jnp.sum(dotted, axis=0, keepdims=True) * inv_total

            def step(g, carry):
                total_qt, total, dotted = carry
                total_qt = grad_group(size, mine, i, g, inv_total, row_delta, total_qt)
                total, dotted = score_group(size, other, later, g, (total, dotted))
                return total_qt, total, dotted

            total_qt, total, dotted = lax.fori_loop(
                0,
                jnp.maximum(groups_of(i, size), groups_of(later, size)),
                step,
                (jnp.zeros((HEAD_DIM, BLOCK), F32), zero, zero),
            )
            grad_qt[i] = total_qt
            return total, dotted

        def two_blocks(step, stats):
            i = first + 2 * step
            stats = query_block(i, i + 1, pairs_even, pairs_odd, stats)
            return query_block(i + 1, jnp.minimum(i + 2, last - 1), pairs_odd, pairs_even, stats)

        lax.fori_loop(0, (last - first) // 2, two_blocks, stats)

    dense = info_ref[3]
    pl.when(dense > 0)(lambda: attend(DENSE_GROUP))
    pl.when(dense == 0)(lambda: attend(SPARSE_GROUP))

    def finish_queries(step, total):
        for u in range(UNROLL):
            i = first + step * UNROLL + u
            grad, gains = norm_back(in_ref[i, 0].astype(F32), q_gain, grad_qt[i].T * SCALE)
            qk_out[i, 0] = grad.astype(BF16)
            total = total + fold_rows(gains)
        return total

    def finish_keys(step, total):
        for u in range(UNROLL):
            j = step * UNROLL + u
            grad, gains = norm_back(in_ref[j, 1].astype(F32), k_gain, acc[j, :, HEAD_DIM:] * SCALE)
            qk_out[j, 1] = grad.astype(BF16)
            v_out[j] = acc[j, :, :HEAD_DIM].astype(BF16)
            total = total + fold_rows(gains)
        for copy in store(step):
            copy.start()
        return total

    part_ref[0:8, :] = lax.fori_loop(0, (last - first) // UNROLL, finish_queries, zero)
    part_ref[8:16, :] = lax.fori_loop(0, nb // UNROLL, finish_keys, zero)
    for step in range(nb // UNROLL):
        for copy in store(step):
            copy.wait()


def item_grads(info, block_list, gains, arrived):
    nb = arrived.shape[0]
    slots = block_list.shape[0] // nb
    smem = pl.BlockSpec(memory_space=pltpu.SMEM)
    vmem = pl.BlockSpec(memory_space=pltpu.VMEM)
    hbm = pl.BlockSpec(memory_space=pltpu.HBM)
    return pl.pallas_call(
        functools.partial(item_kernel, nb),
        out_shape=(
            jax.ShapeDtypeStruct((nb, 2, BLOCK, HEAD_DIM), BF16),
            jax.ShapeDtypeStruct((nb, BLOCK, HEAD_DIM), BF16),
            jax.ShapeDtypeStruct((16, HEAD_DIM), F32),
        ),
        in_specs=[smem, smem, vmem, hbm],
        out_specs=(hbm, hbm, vmem),
        scratch_shapes=[
            pltpu.VMEM((nb, 4, BLOCK, HEAD_DIM), BF16),
            pltpu.VMEM((nb, 2, BLOCK, HEAD_DIM), BF16),
            pltpu.VMEM((nb, BLOCK, HEAD_DIM), BF16),
            pltpu.SemaphoreType.DMA((nb // UNROLL,)),
            pltpu.SemaphoreType.DMA((nb // UNROLL,)),
            pltpu.SemaphoreType.DMA((nb // UNROLL,)),
            pltpu.VMEM((nb + 1, BLOCK, 2 * HEAD_DIM), BF16),
            pltpu.VMEM((nb + 1, HEAD_DIM, BLOCK), BF16),
            pltpu.VMEM((slots, BLOCK, 2 * BLOCK), F32),
            pltpu.VMEM((slots, BLOCK, 2 * BLOCK), F32),
            pltpu.VMEM((nb + 1, BLOCK, 2 * HEAD_DIM), F32),
            pltpu.VMEM((nb, 2 * HEAD_DIM, 2 * BLOCK), BF16),
            pltpu.VMEM((nb, 2 * BLOCK, 2 * HEAD_DIM), BF16),
            pltpu.VMEM((nb, HEAD_DIM, BLOCK), F32),
            pltpu.VMEM((nb, 8, BLOCK), F32),
        ],
        compiler_params=pltpu.CompilerParams(vmem_limit_bytes=60 * 2**20),
        name="item_grads",
    )(info, block_list, gains, arrived)


def merge_kernel(count, heads_ref, in_ref, *out_refs):
    outs = out_refs[:count]

    def piece(slot, which):
        return in_ref[slot, which * BLOCK : (which + 1) * BLOCK, :]

    def pair(p, carry):
        at = pl.multiple_of(heads_ref[2 * p] * HEAD_DIM, HEAD_DIM)
        for which, out in enumerate(outs):
            both = piece(2 * p, which).astype(F32) + piece(2 * p + 1, which).astype(F32)
            out[:, pl.ds(at, HEAD_DIM)] = both.astype(BF16)
        return carry

    def single(slot, carry):
        at = pl.multiple_of(heads_ref[slot] * HEAD_DIM, HEAD_DIM)
        for which, out in enumerate(outs):
            out[:, pl.ds(at, HEAD_DIM)] = piece(slot, which)
        return carry

    lax.fori_loop(0, SPLITS, pair, 0)
    lax.fori_loop(2 * SPLITS, ITEMS, single, 0)
    if len(out_refs) > count:
        def tail(slot, total):
            return total + in_ref[slot, count * BLOCK : count * BLOCK + 16, :].astype(F32)

        total = lax.fori_loop(0, ITEMS, tail, jnp.zeros((16, HEAD_DIM), F32))
        out_refs[count][...] = total[0:2] + (total[2:4] + total[4:6])


def merge(item_heads, returned, count, with_tail):
    vmem = pl.BlockSpec(memory_space=pltpu.VMEM)
    wide = jax.ShapeDtypeStruct((BLOCK, HEADS * HEAD_DIM), BF16)
    shapes = (wide,) * count + ((jax.ShapeDtypeStruct((2, HEAD_DIM), F32),) if with_tail else ())
    return pl.pallas_call(
        functools.partial(merge_kernel, count),
        out_shape=shapes,
        in_specs=[pl.BlockSpec(memory_space=pltpu.SMEM), vmem],
        out_specs=(vmem,) * len(shapes),
        compiler_params=pltpu.CompilerParams(vmem_limit_bytes=24 * 2**20),
        name="merge_heads",
    )(item_heads, returned)


def attach_kernel(part_ref, v_ref, out_ref):
    total = part_ref[...]
    high = total.astype(BF16)
    rest = total - high.astype(F32)
    middle = rest.astype(BF16)
    low = (rest - middle.astype(F32)).astype(BF16)
    pieces = [high.astype(F32), middle.astype(F32), low.astype(F32), jnp.zeros((10, HEAD_DIM), F32)]
    tail = jnp.concatenate(pieces, axis=0).astype(BF16)

    def move(slot, carry):
        out_ref[slot, :BLOCK, :] = v_ref[slot]
        out_ref[slot, BLOCK:, :] = tail
        return carry

    lax.fori_loop(0, ITEMS, move, 0)


def attach(part, grads_v):
    vmem = pl.BlockSpec(memory_space=pltpu.VMEM)
    return pl.pallas_call(
        attach_kernel,
        out_shape=jax.ShapeDtypeStruct((ITEMS, BLOCK + 16, HEAD_DIM), BF16),
        in_specs=[vmem, vmem],
        out_specs=vmem,
        name="attach_gains",
    )(part, grads_v)


def sum_over_videos(part):
    count = lax.axis_size("dp")
    step = 1
    while step < count:
        part = part + lax.ppermute(part, "dp", [(i, i ^ step) for i in range(count)])
        step *= 2
    return part


def plan_items(block_masks):
    totals = jnp.sum((block_masks > 0).astype(jnp.int32), axis=(1, 2))
    heads = jnp.arange(HEADS, dtype=jnp.int32)
    ahead = (totals[None, :] > totals[:, None]) | (
        (totals[None, :] == totals[:, None]) & (heads[None, :] < heads[:, None])
    )
    rank = jnp.sum(ahead.astype(jnp.int32), axis=1)
    counter = jnp.arange(ITEMS, dtype=jnp.int32)
    wanted = jnp.where(counter < 2 * SPLITS, counter // 2, counter - SPLITS)
    return jnp.sum(jnp.where(rank[None, :] == wanted[:, None], heads[None, :], 0), axis=1)


def block_lists(mask_head):
    nb = mask_head.shape[0]
    on = (mask_head > 0).astype(jnp.int32)
    lower = (jnp.arange(nb)[:, None] < jnp.arange(nb)[None, :]).astype(jnp.int32)
    place = jnp.sum(on[:, :, None] * lower[None, :, :], axis=1)
    slot = jnp.arange(nb, dtype=jnp.int32)
    hit = (on[:, :, None] > 0) & (place[:, :, None] == slot[None, None, :])
    which = jnp.arange(nb, dtype=jnp.int32)[None, :, None]
    counts = jnp.sum(on, axis=1)
    lists = nb + jnp.sum(jnp.where(hit, which - nb, 0), axis=1)
    return counts, lists


def body(q_raw, k_raw, values, grad_out, q_gain, k_gain, block_masks):
    device_rank = lax.axis_index("ulysses")
    tok_rows, width = q_raw.shape[1:]
    nb = block_masks.shape[1]
    seq_len = tok_rows * lax.axis_size("ulysses")
    videos = lax.axis_size("dp")
    item_heads = plan_items(block_masks)
    outgoing = pack(item_heads, q_raw[0], k_raw[0], values[0], grad_out[0])
    arrived = lax.all_to_all(outgoing, "ulysses", split_axis=0, concat_axis=0, tiled=True)
    head = lax.dynamic_index_in_dim(item_heads, device_rank, 0, keepdims=False)
    counts, lists = block_lists(lax.dynamic_index_in_dim(block_masks, head, 0, keepdims=False))
    split = device_rank < 2 * SPLITS
    half = device_rank % 2
    first = jnp.where(split, half * (nb // 2), 0)
    last = jnp.where(split, (half + 1) * (nb // 2), nb)
    bound = 1.02 * HEAD_DIM * SCORE2 * jnp.max(jnp.abs(q_gain)) * jnp.max(jnp.abs(k_gain))
    careful = jnp.where(bound < SAFE_BOUND, 0, 1)
    dense = jnp.where(jnp.max(counts) > DENSE_FROM, 1, 0)
    info = jnp.concatenate(
        [jnp.stack([first, last, careful, dense]).astype(jnp.int32), jnp.zeros((4,), jnp.int32), counts]
    )
    gains = jnp.stack([q_gain, k_gain])
    grads_qk, grads_v, part = item_grads(info, lists.reshape(-1), gains, arrived)
    back_qk = lax.all_to_all(
        grads_qk.reshape(nb, 2 * BLOCK, HEAD_DIM), "ulysses", split_axis=0, concat_axis=0, tiled=True
    )
    part = sum_over_videos(jnp.sum(part.reshape(2, 8, HEAD_DIM), axis=1))
    attached, back_qk = lax.optimization_barrier((attach(part, grads_v), back_qk))
    back_v = lax.all_to_all(attached, "ulysses", split_axis=0, concat_axis=0, tiled=True)
    grad_q, grad_k = merge(item_heads, back_qk, 2, False)
    grad_v, summed = merge(item_heads, back_v, 1, True)
    gain_grads = summed * (videos * seq_len * HEADS) ** (-0.5)
    return (grad_q[None], grad_k[None], grad_v[None], gain_grads)


def solution(mesh):
    tokens = P("dp", "ulysses", None)
    return jax.shard_map(
        body,
        mesh=mesh,
        in_specs=(tokens, tokens, tokens, tokens, P(), P(), P()),
        out_specs=(tokens, tokens, tokens, P()),
        check_vma=False,
    )
```

time: 313 us -> 231 us (0.74)
  blocking collectives: 107 us -> 0 us
  waiting for transfers between devices: 43.5 us -> 70.3 us
  starting transfers between devices: 12.6 us -> 30.9 us
  Pallas kernels: 130 us -> 115 us
  local copies, waits for them, and re-layouts: 8.91 us -> 1.86 us
    psum x1 -> x0, blocking collectives: 107 us -> none  [body(): lax.psum(jnp.sum(part.reshape(2, 8, HEAD_DIM), axis=1), ('dp', 'ulysses'))]
    all_to_all x1 -> x2, waiting for transfers between devices: 0.01 us -> 26 us  [the longest x1 15.6 us: body(): lax.all_to_all(attached, 'ulysses', split_axis=0, concat_axis=0, tiled=True)]
    pallas_call x1, Pallas kernels: 126 us -> 104 us  [item_grads(): pl.pallas_call(functools.partial(item_kernel, nb), out_shape=(jax.ShapeDt...]
    ppermute x0 -> x3, starting transfers between devices: none -> 10.8 us  [sum_over_videos(): lax.ppermute(part, 'dp', [(i, i ^ step) for i in range(count)])]
    unnamed x16 -> x8, local copies, waits for them, and re-layouts: 8.16 us -> 0.03 us
    all_to_all x1 -> x2, starting transfers between devices: 3.85 us -> 11.3 us  [the longest x1 5.96 us: body(): lax.all_to_all(attached, 'ulysses', split_axis=0, concat_axis=0, tiled=True)]
    pallas_call x1 -> x3, Pallas kernels: 2.68 us -> 6.5 us  [the longest x2 4.05 us: merge(): pl.pallas_call(functools.partial(merge_kernel, count), out_shape=shapes,...]
    ppermute x0 -> x3, waiting for transfers between devices: none -> 3.76 us  [sum_over_videos(): lax.ppermute(part, 'dp', [(i, i ^ step) for i in range(count)])]
  transfers between devices with their start and end apart: 2 -> 6, of which waited for: 1 -> 6; matrix products, arithmetic and copies ran while one was open for 1% -> 3% of each run, Pallas kernels for 0% -> 2%
where the time goes in v2:
time: 231 us; the launch traced here: 230 us
  Pallas kernels  115 us (50%)
  waiting for transfers between devices  70.3 us (30%)
  starting transfers between devices  30.9 us (13%)
  other arithmetic  7.33 us (3%)
  between operations  4.72 us (2%)
    pallas_call x1, Pallas kernels, item_grads(): pl.pallas_call(functools.partial(item_kernel, nb), out_shape=(jax.ShapeDt...  104 us
    all_to_all x1, waiting for transfers between devices, body(): lax.all_to_all(outgoing, 'ulysses', split_axis=0, concat_axis=0, tiled=True)  40.6 us
    all_to_all x1, waiting for transfers between devices, body(): lax.all_to_all(attached, 'ulysses', split_axis=0, concat_axis=0, tiled=True)  15.6 us
    ppermute x3, starting transfers between devices, sum_over_videos(): lax.ppermute(part, 'dp', [(i, i ^ step) for i in range(count)])  10.8 us
    all_to_all x1, waiting for transfers between devices, body(): lax.all_to_all(grads_qk.reshape(nb, 2 * BLOCK, HEAD_DIM), 'ulysses', spli...  10.3 us
    all_to_all x1, starting transfers between devices, body(): lax.all_to_all(outgoing, 'ulysses', split_axis=0, concat_axis=0, tiled=True)  8.79 us
    all_to_all x1, starting transfers between devices, body(): lax.all_to_all(attached, 'ulysses', split_axis=0, concat_axis=0, tiled=True)  5.96 us
    all_to_all x1, starting transfers between devices, body(): lax.all_to_all(grads_qk.reshape(nb, 2 * BLOCK, HEAD_DIM), 'ulysses', spli...  5.32 us
  transfers between devices with their start and end apart: 6, of which 6 were waited for; matrix products, arithmetic and copies ran while one was open for 3% of the time, Pallas kernels for 2%

profile of v2, /device:TPU:1, one launch (start us, length us, event | category | flops | bytes accessed | tf_op | source)
XLA Modules:
  0.0 230.3 jit_solution(11212179379816574170)
XLA Ops:
  0.6 1.5 convert_reduce_fusion
  2.2 0.2 convert_reduce_fusion.2
  2.4 0.6 select_reduce_fusion.1.heads_ref
  3.0 4.9 %pack_heads.1 = bf16[32,4,128,128]{3,2,1,0:T(8,128)(2,1)} custom-call(s32[32]{0:T(128)} %select_reduce_fusion.1.heads_ref, bf16[128,3072]{1,0:T(8,128)(2,1)} %bitcast.22, bf16[128,3072]{1,0:T(8,128)(2,1)} %bitcast.23, bf16[128,3072]{1,0:T(8,128)(2,1)} %bitcast.24, bf16[128,3072]{1,0:T(8,128)(2,1)} %bitcast.25), custom_call_target="tpu_custom_call" | custom-call | tf_op jit(solution)/shard_map/pack_heads/pallas_call | solution.py:61
  7.8 0.0 copy-start
  7.8 0.0 copy-start.2
  7.9 0.0 copy-start.3
  7.9 8.8 %all-to-all-start = ((bf16[32,4,128,128]{3,2,1,0:T(8,128)(2,1)}), bf16[32,4,128,128]{3,2,1,0:T(8,128)(2,1)}, u32[]{:S(2)}, u32[]{:S(2)}) async-start(bf16[32,4,128,128]{3,2,1,0:T(8,128)(2,1)} %pack_heads.1), calls=%async_computation | async-start | bytes 8388608 | tf_op jit(solution)/shard_map/all_to_all | solution.py:422
  16.7 0.0 copy-done
  16.7 0.6 dynamic_slice.8
  19.2 0.7 broadcast_compare_fusion
  20.0 0.2 multiply_reduce_fusion
  20.2 0.4 select_reduce_fusion
  20.6 0.7 add.56.list_ref
  21.3 0.1 convert_reduce_fusion.1
  21.4 0.6 reduce_max.29
  22.7 0.0 copy-done.2
  22.7 0.6 abs_reduce_fusion.1
  23.9 0.0 copy-done.3
  23.9 0.6 abs_reduce_fusion
  25.2 0.6 concatenate.3.info_ref
  25.8 0.6 pad_maximum_fusion.gain_ref
  26.3 40.6 %all-to-all-done.hbm_ref = bf16[32,4,128,128]{3,2,1,0:T(8,128)(2,1)} async-done(((bf16[32,4,128,128]{3,2,1,0:T(8,128)(2,1)}), bf16[32,4,128,128]{3,2,1,0:T(8,128)(2,1)}, u32[]{:S(2)}, u32[]{:S(2)}) %all-to-all-start) | async-done | bytes 4194336 | tf_op jit(solution)/shard_map/all_to_all | solution.py:422
  66.9 103.9 %item_grads.1 = (bf16[32,2,128,128]{3,2,1,0:T(8,128)(2,1)}, bf16[32,128,128]{2,1,0:T(8,128)(2,1)}, f32[16,128]{1,0:T(8,128)}) custom-call(s32[40]{0:T(128)} %concatenate.3.info_ref, s32[1024]{0:T(1024)} %add.56.list_ref, f32[2,128]{1,0:T(2,128)} %pad_maximum_fusion.gain_ref, bf16[32,4,128,128]{3,2,1,0:T(8,128)(2,1)} %all-to-all-done.hbm_ref), custom_call_target="tpu_custom_call" | custom-call | tf_op jit(solution)/shard_map/item_grads/pallas_call | solution.py:278
  170.8 0.0 copy-start.1
  170.8 5.3 %all-to-all-start.1 = ((bf16[32,256,128]{2,1,0:T(8,128)(2,1)}), bf16[32,256,128]{2,1,0:T(8,128)(2,1)S(1)}, u32[]{:S(2)}, u32[]{:S(2)}) async-start(bf16[32,256,128]{2,1,0:T(8,128)(2,1)} %bitcast.21), calls=%async_computation.1 | async-start | bytes 4194304 | tf_op jit(solution)/shard_map/all_to_all | solution.py:437
  176.2 0.0 copy-done.1
  176.2 1.7 collective-permute-start
  177.9 1.3 collective-permute-done
  179.2 3.0 %collective-permute-start.1 = (f32[2,128]{1,0:T(2,128)S(1)}, f32[2,128]{1,0:T(2,128)S(1)}, u32[]{:S(2)}, u32[]{:S(2)}) collective-permute-start(f32[2,128]{1,0:T(2,128)S(1)} %add.57), channel_id=1, source_target_pairs={{0,64},{32,96},{64,0},{96,32},{128,192},{160,224},{192,128},{224,1... | collective-permute-start | bytes 3080 | tf_op jit(solution)/shard_map/ppermute | solution.py:384
  182.2 1.3 collective-permute-done.1
  183.4 6.1 %collective-permute-start.2 = (f32[2,128]{1,0:T(2,128)S(1)}, f32[2,128]{1,0:T(2,128)S(1)}, u32[]{:S(2)}, u32[]{:S(2)}) collective-permute-start(f32[2,128]{1,0:T(2,128)S(1)} %add.58), channel_id=1, source_target_pairs={{0,128},{32,160},{64,192},{96,224},{128,0},{160,32},{192,64},{224,... | collective-permute-start | bytes 3080 | tf_op jit(solution)/shard_map/ppermute | solution.py:384
  189.5 1.3 collective-permute-done.2
  190.8 0.6 add.59.part_ref
  191.3 2.5 %attach_gains.1 = bf16[32,144,128]{2,1,0:T(8,128)(2,1)} custom-call(f32[2,128]{1,0:T(2,128)} %add.59.part_ref, bf16[32,128,128]{2,1,0:T(8,128)(2,1)} %get-tuple-element.14.v_ref), custom_call_target="tpu_custom_call" | custom-call | tf_op jit(solution)/shard_map/attach_gains/pallas_call | solution.py:371
  193.8 10.3 %all-to-all-done.1.in_ref = bf16[32,256,128]{2,1,0:T(8,128)(2,1)S(1)} async-done(((bf16[32,256,128]{2,1,0:T(8,128)(2,1)}), bf16[32,256,128]{2,1,0:T(8,128)(2,1)S(1)}, u32[]{:S(2)}, u32[]{:S(2)}) %all-to-all-start.1) | async-done | bytes 2097184 | tf_op jit(solution)/shard_map/all_to_all | solution.py:437
  204.1 6.0 %all-to-all-start.2 = ((bf16[32,144,128]{2,1,0:T(8,128)(2,1)}), bf16[32,144,128]{2,1,0:T(8,128)(2,1)S(1)}, u32[]{:S(2)}, u32[]{:S(2)}) async-start(bf16[32,144,128]{2,1,0:T(8,128)(2,1)} %attach_gains.1), calls=%async_computation.2 | async-start | bytes 2359296 | tf_op jit(solution)/shard_map/all_to_all | solution.py:442
  210.1 2.2 merge_heads.2
  212.3 15.6 %all-to-all-done.2.in_ref = bf16[32,144,128]{2,1,0:T(8,128)(2,1)S(1)} async-done(((bf16[32,144,128]{2,1,0:T(8,128)(2,1)}), bf16[32,144,128]{2,1,0:T(8,128)(2,1)S(1)}, u32[]{:S(2)}, u32[]{:S(2)}) %all-to-all-start.2) | async-done | bytes 1179680 | tf_op jit(solution)/shard_map/all_to_all | solution.py:442
  227.9 1.9 merge_heads.3
  229.7 0.6 broadcast_multiply_fusion
  (9 shorter events, 0.0 us)
Async XLA Ops:
  7.8 8.8 %copy-start = (s32[32]{0:T(128)S(1)}, s32[32]{0:T(128)}, u32[]{:S(2)}) copy-start(s32[32]{0:T(128)} %select_reduce_fusion.1.heads_ref) | copy-start | bytes 388
  7.8 14.8 %copy-start.2 = (f32[128]{0:T(128)S(1)}, f32[128]{0:T(128)}, u32[]{:S(2)}) copy-start(f32[128]{0:T(128)} %param.11) | copy-start | bytes 1540
  7.9 16.1 %copy-start.3 = (f32[128]{0:T(128)S(1)}, f32[128]{0:T(128)}, u32[]{:S(2)}) copy-start(f32[128]{0:T(128)} %param.12) | copy-start | bytes 1540
  7.9 59.1 %all-to-all-start = ((bf16[32,4,128,128]{3,2,1,0:T(8,128)(2,1)}), bf16[32,4,128,128]{3,2,1,0:T(8,128)(2,1)}, u32[]{:S(2)}, u32[]{:S(2)}) async-start(bf16[32,4,128,128]{3,2,1,0:T(8,128)(2,1)} %pack_heads.1), calls=%async_computation | async-start | bytes 8388608 | tf_op jit(solution)/shard_map/all_to_all | solution.py:422
  170.8 5.3 %copy-start.1 = (f32[16,128]{1,0:T(8,128)S(1)}, f32[16,128]{1,0:T(8,128)}, u32[]{:S(2)}) copy-start(f32[16,128]{1,0:T(8,128)} %get-tuple-element.13) | copy-start | bytes 24580
  170.8 33.3 %all-to-all-start.1 = ((bf16[32,256,128]{2,1,0:T(8,128)(2,1)}), bf16[32,256,128]{2,1,0:T(8,128)(2,1)S(1)}, u32[]{:S(2)}, u32[]{:S(2)}) async-start(bf16[32,256,128]{2,1,0:T(8,128)(2,1)} %bitcast.21), calls=%async_computation.1 | async-start | bytes 4194304 | tf_op jit(solution)/shard_map/all_to_all | solution.py:437
  176.2 3.0 %collective-permute-start = (f32[2,128]{1,0:T(2,128)S(1)}, f32[2,128]{1,0:T(2,128)S(1)}, u32[]{:S(2)}, u32[]{:S(2)}) collective-permute-start(f32[2,128]{1,0:T(2,128)S(1)} %bitcast_reduce_fusion), channel_id=1, source_target_pairs={{0,32},{32,0},{64,96},{96,64},{128,160},{160,128},{192,224},{224,1... | collective-permute-start | bytes 3080 | tf_op jit(solution)/shard_map/ppermute | solution.py:384
  179.2 4.3 %collective-permute-start.1 = (f32[2,128]{1,0:T(2,128)S(1)}, f32[2,128]{1,0:T(2,128)S(1)}, u32[]{:S(2)}, u32[]{:S(2)}) collective-permute-start(f32[2,128]{1,0:T(2,128)S(1)} %add.57), channel_id=1, source_target_pairs={{0,64},{32,96},{64,0},{96,32},{128,192},{160,224},{192,128},{224,1... | collective-permute-start | bytes 3080 | tf_op jit(solution)/shard_map/ppermute | solution.py:384
  183.4 7.3 %collective-permute-start.2 = (f32[2,128]{1,0:T(2,128)S(1)}, f32[2,128]{1,0:T(2,128)S(1)}, u32[]{:S(2)}, u32[]{:S(2)}) collective-permute-start(f32[2,128]{1,0:T(2,128)S(1)} %add.58), channel_id=1, source_target_pairs={{0,128},{32,160},{64,192},{96,224},{128,0},{160,32},{192,64},{224,... | collective-permute-start | bytes 3080 | tf_op jit(solution)/shard_map/ppermute | solution.py:384
  204.1 23.8 %all-to-all-start.2 = ((bf16[32,144,128]{2,1,0:T(8,128)(2,1)}), bf16[32,144,128]{2,1,0:T(8,128)(2,1)S(1)}, u32[]{:S(2)}, u32[]{:S(2)}) async-start(bf16[32,144,128]{2,1,0:T(8,128)(2,1)} %attach_gains.1), calls=%async_computation.2 | async-start | bytes 2359296 | tf_op jit(solution)/shard_map/all_to_all | solution.py:442

commit v3 on v2

--- a/solution.py
+++ b/solution.py
@@ -12,8 +12,7 @@
 SPLITS = 8
 BLOCK = 128
 ITEMS = 32
-DENSE_GROUP = 16
-SPARSE_GROUP = 4
+GROUP = 5
 DENSE_FROM = 12
 CHUNK = 4
 UNROLL = 4
@@ -91,7 +90,7 @@
 
 
 def item_kernel(
-    nb, info_ref, list_ref, gain_ref, hbm_ref, qk_ref, v_ref, part_ref,
+    nb, info_ref, list_ref, mask_ref, gain_ref, hbm_ref, qk_ref, v_ref, part_ref,
     in_ref, qk_out, v_out, in_sems, qk_sems, v_sems, kv, kt, pairs_even, pairs_odd, acc, left, right, grad_qt, shifts,
 ):
     first, last, careful = info_ref[0], info_ref[1], info_ref[2]
@@ -150,12 +149,6 @@
     kt[nb] = zero_half
     acc[nb] = jnp.zeros((BLOCK, 2 * HEAD_DIM), F32)
 
-    def clear(at, carry):
-        pairs_even[at] = jnp.zeros((BLOCK, 2 * BLOCK), F32)
-        pairs_odd[at] = jnp.zeros((BLOCK, 2 * BLOCK), F32)
-        return carry
-
-    lax.fori_loop(0, slots, clear, 0)
     part_ref[...] = jnp.zeros((16, HEAD_DIM), F32)
 
     @pl.when(careful > 0)
@@ -172,17 +165,12 @@
 
         lax.fori_loop(first, last, peak_row, 0)
 
-    def groups_of(i, size):
-        return (info_ref[8 + i] + (size - 1)) // size
-
-    def score_group(size, pairs, i, g, stats):
+    def score_group(pairs, i, places, stats):
         total, dotted = stats
-        count = info_ref[8 + i]
         shift = shifts[i, 0:1, :]
-        for u in range(size):
-            at = g * size + u
-            both = jnp.dot(kv[list_ref[i * slots + at]], left[i], preferred_element_type=F32)
-            weights = jnp.exp2(both[:, :BLOCK] * SCORE2 + (jnp.where(at < count, 0.0, NEG_FILL) - shift))
+        for at, j, allowed in places:
+            both = jnp.dot(kv[j], left[i], preferred_element_type=F32)
+            weights = jnp.exp2(both[:, :BLOCK] * SCORE2 + (jnp.where(allowed, 0.0, NEG_FILL) - shift))
             grads = both[:, BLOCK:]
             pairs[at, :, :BLOCK] = weights
             pairs[at, :, BLOCK:] = grads
@@ -190,11 +178,9 @@
             dotted = dotted + fold_rows(weights * grads)
         return total, dotted
 
-    def grad_group(size, pairs, i, g, inv_total, row_delta, total_qt):
+    def grad_group(pairs, i, places, inv_total, row_delta, total_qt):
         halves, keys = [], []
-        for u in range(size):
-            at = g * size + u
-            j = list_ref[i * slots + at]
+        for at, j, _ in places:
             weights = pairs[at, :, :BLOCK] * inv_total
             half = (weights * (pairs[at, :, BLOCK:] - row_delta)).astype(BF16)
             acc[j] += jnp.dot(
@@ -207,31 +193,14 @@
         )
 
     zero = jnp.zeros((8, BLOCK), F32)
-    def attend(size):
-        stats = lax.fori_loop(
-            0, groups_of(first, size), lambda g, s: score_group(size, pairs_even, first, g, s), (zero, zero)
-        )
-
-        def query_block(i, later, mine, other, stats):
-            total, dotted = stats
-            inv_total = 1.0 / jnp.sum(total, axis=0, keepdims=True)
-            row_delta = jnp.sum(dotted, axis=0, keepdims=True) * inv_total
-
-            def step(g, carry):
-                total_qt, total, dotted = carry
-                total_qt = grad_group(size, mine, i, g, inv_total, row_delta, total_qt)
-                total, dotted = score_group(size, other, later, g, (total, dotted))
-                return total_qt, total, dotted
-
-            total_qt, total, dotted = lax.fori_loop(
-                0,
-                jnp.maximum(groups_of(i, size), groups_of(later, size)),
-                step,
-                (jnp.zeros((HEAD_DIM, BLOCK), F32), zero, zero),
-            )
-            grad_qt[i] = total_qt
-            return total, dotted
-
+    no_grad = jnp.zeros((HEAD_DIM, BLOCK), F32)
+
+    def row_scales(stats):
+        total, dotted = stats
+        inv_total = 1.0 / jnp.sum(total, axis=0, keepdims=True)
+        return inv_total, jnp.sum(dotted, axis=0, keepdims=True) * inv_total
+
+    def rows_in_turn(stats, query_block):
         def two_blocks(step, stats):
             i = first + 2 * step
             stats = query_block(i, i + 1, pairs_even, pairs_odd, stats)
@@ -239,9 +208,54 @@
 
         lax.fori_loop(0, (last - first) // 2, two_blocks, stats)
 
+    def attend_all():
+        def places(i):
+            return [(j, j, mask_ref[i * nb + j] > 0) for j in range(nb)]
+
+        def query_block(i, later, mine, other, stats):
+            inv_total, row_delta = row_scales(stats)
+            grad_qt[i] = grad_group(mine, i, places(i), inv_total, row_delta, no_grad)
+            return score_group(other, later, places(later), (zero, zero))
+
+        rows_in_turn(score_group(pairs_even, first, places(first), (zero, zero)), query_block)
+
+    def attend_listed():
+        def clear(at, carry):
+            pairs_even[at] = jnp.zeros((BLOCK, 2 * BLOCK), F32)
+            pairs_odd[at] = jnp.zeros((BLOCK, 2 * BLOCK), F32)
+            return carry
+
+        lax.fori_loop(0, slots, clear, 0)
+
+        def groups_of(i):
+            return (info_ref[8 + i] + (GROUP - 1)) // GROUP
+
+        def places(i, g):
+            spots = [g * GROUP + u for u in range(GROUP)]
+            return [(at, list_ref[i * slots + at], at < info_ref[8 + i]) for at in spots]
+
+        def query_block(i, later, mine, other, stats):
+            inv_total, row_delta = row_scales(stats)
+
+            def step(g, carry):
+                total_qt, total, dotted = carry
+                total_qt = grad_group(mine, i, places(i, g), inv_total, row_delta, total_qt)
+                return (total_qt, *score_group(other, later, places(later, g), (total, dotted)))
+
+            total_qt, total, dotted = lax.fori_loop(
+                0, jnp.maximum(groups_of(i), groups_of(later)), step, (no_grad, zero, zero)
+            )
+            grad_qt[i] = total_qt
+            return total, dotted
+
+        stats = lax.fori_loop(
+            0, groups_of(first), lambda g, s: score_group(pairs_even, first, places(first, g), s), (zero, zero)
+        )
+        rows_in_turn(stats, query_block)
+
     dense = info_ref[3]
-    pl.when(dense > 0)(lambda: attend(DENSE_GROUP))
-    pl.when(dense == 0)(lambda: attend(SPARSE_GROUP))
+    pl.when(dense > 0)(attend_all)
+    pl.when(dense == 0)(attend_listed)
 
     def finish_queries(step, total):
         for u in range(UNROLL):
@@ -269,7 +283,7 @@
             copy.wait()
 
 
-def item_grads(info, block_list, gains, arrived):
+def item_grads(info, block_list, mask, gains, arrived):
     nb = arrived.shape[0]
     slots = block_list.shape[0] // nb
     smem = pl.BlockSpec(memory_space=pltpu.SMEM)
@@ -282,7 +296,7 @@
             jax.ShapeDtypeStruct((nb, BLOCK, HEAD_DIM), BF16),
             jax.ShapeDtypeStruct((16, HEAD_DIM), F32),
         ),
-        in_specs=[smem, smem, vmem, hbm],
+        in_specs=[smem, smem, smem, vmem, hbm],
         out_specs=(hbm, hbm, vmem),
         scratch_shapes=[
             pltpu.VMEM((nb, 4, BLOCK, HEAD_DIM), BF16),
@@ -303,10 +317,10 @@
         ],
         compiler_params=pltpu.CompilerParams(vmem_limit_bytes=60 * 2**20),
         name="item_grads",
-    )(info, block_list, gains, arrived)
-
-
-def merge_kernel(count, heads_ref, in_ref, *out_refs):
+    )(info, block_list, mask, gains, arrived)
+
+
+def merge_kernel(count, tail_scale, heads_ref, in_ref, *out_refs):
     outs = out_refs[:count]
 
     def piece(slot, which):
@@ -332,15 +346,15 @@
             return total + in_ref[slot, count * BLOCK : count * BLOCK + 16, :].astype(F32)
 
         total = lax.fori_loop(0, ITEMS, tail, jnp.zeros((16, HEAD_DIM), F32))
-        out_refs[count][...] = total[0:2] + (total[2:4] + total[4:6])
-
-
-def merge(item_heads, returned, count, with_tail):
+        out_refs[count][...] = (total[0:2] + (total[2:4] + total[4:6])) * tail_scale
+
+
+def merge(item_heads, returned, count, tail_scale=None):
     vmem = pl.BlockSpec(memory_space=pltpu.VMEM)
     wide = jax.ShapeDtypeStruct((BLOCK, HEADS * HEAD_DIM), BF16)
-    shapes = (wide,) * count + ((jax.ShapeDtypeStruct((2, HEAD_DIM), F32),) if with_tail else ())
+    shapes = (wide,) * count + ((jax.ShapeDtypeStruct((2, HEAD_DIM), F32),) if tail_scale else ())
     return pl.pallas_call(
-        functools.partial(merge_kernel, count),
+        functools.partial(merge_kernel, count, tail_scale),
         out_shape=shapes,
         in_specs=[pl.BlockSpec(memory_space=pltpu.SMEM), vmem],
         out_specs=(vmem,) * len(shapes),
@@ -421,7 +435,8 @@
     outgoing = pack(item_heads, q_raw[0], k_raw[0], values[0], grad_out[0])
     arrived = lax.all_to_all(outgoing, "ulysses", split_axis=0, concat_axis=0, tiled=True)
     head = lax.dynamic_index_in_dim(item_heads, device_rank, 0, keepdims=False)
-    counts, lists = block_lists(lax.dynamic_index_in_dim(block_masks, head, 0, keepdims=False))
+    mask_head = lax.dynamic_index_in_dim(block_masks, head, 0, keepdims=False)
+    counts, lists = block_lists(mask_head)
     split = device_rank < 2 * SPLITS
     half = device_rank % 2
     first = jnp.where(split, half * (nb // 2), 0)
@@ -433,16 +448,15 @@
         [jnp.stack([first, last, careful, dense]).astype(jnp.int32), jnp.zeros((4,), jnp.int32), counts]
     )
     gains = jnp.stack([q_gain, k_gain])
-    grads_qk, grads_v, part = item_grads(info, lists.reshape(-1), gains, arrived)
+    grads_qk, grads_v, part = item_grads(info, lists.reshape(-1), mask_head.reshape(-1), gains, arrived)
     back_qk = lax.all_to_all(
         grads_qk.reshape(nb, 2 * BLOCK, HEAD_DIM), "ulysses", split_axis=0, concat_axis=0, tiled=True
     )
     part = sum_over_videos(jnp.sum(part.reshape(2, 8, HEAD_DIM), axis=1))
     attached, back_qk = lax.optimization_barrier((attach(part, grads_v), back_qk))
     back_v = lax.all_to_all(attached, "ulysses", split_axis=0, concat_axis=0, tiled=True)
-    grad_q, grad_k = merge(item_heads, back_qk, 2, False)
-    grad_v, summed = merge(item_heads, back_v, 1, True)
-    gain_grads = summed * (videos * seq_len * HEADS) ** (-0.5)
+    grad_q, grad_k = merge(item_heads, back_qk, 2)
+    grad_v, gain_grads = merge(item_heads, back_v, 1, (videos * seq_len * HEADS) ** (-0.5))
     return (grad_q[None], grad_k[None], grad_v[None], gain_grads)
 
 

time: 231 us -> 227 us (0.983)
  Pallas kernels: 115 us -> 108 us
  starting transfers between devices: 30.9 us -> 36.2 us
    pallas_call x1, Pallas kernels: 104 us -> 96.4 us  [item_grads(): pl.pallas_call(functools.partial(item_kernel, nb), out_shape=(jax.ShapeDt...]
    all_to_all x1, starting transfers between devices: 5.32 us -> 10.6 us  [body(): lax.all_to_all(grads_qk.reshape(nb, 2 * BLOCK, HEAD_DIM), 'ulysses', spli...]
where the time goes in v3:
time: 227 us; the launch traced here: 228 us
  Pallas kernels  108 us (48%)
  waiting for transfers between devices  69.7 us (31%)
  starting transfers between devices  36.2 us (16%)
  other arithmetic  6.76 us (3%)
  between operations  4.71 us (2%)
  local copies, waits for them, and re-layouts  2.52 us (1%)
    pallas_call x1, Pallas kernels, item_grads(): pl.pallas_call(functools.partial(item_kernel, nb), out_shape=(jax.ShapeDt...  96.4 us
    all_to_all x1, waiting for transfers between devices, body(): lax.all_to_all(outgoing, 'ulysses', split_axis=0, concat_axis=0, tiled=True)  39.9 us
    all_to_all x1, waiting for transfers between devices, body(): lax.all_to_all(attached, 'ulysses', split_axis=0, concat_axis=0, tiled=True)  15.6 us
    ppermute x3, starting transfers between devices, sum_over_videos(): lax.ppermute(part, 'dp', [(i, i ^ step) for i in range(count)])  10.8 us
    all_to_all x1, starting transfers between devices, body(): lax.all_to_all(grads_qk.reshape(nb, 2 * BLOCK, HEAD_DIM), 'ulysses', spli...  10.6 us
    all_to_all x1, waiting for transfers between devices, body(): lax.all_to_all(grads_qk.reshape(nb, 2 * BLOCK, HEAD_DIM), 'ulysses', spli...  10.3 us
    all_to_all x1, starting transfers between devices, body(): lax.all_to_all(outgoing, 'ulysses', split_axis=0, concat_axis=0, tiled=True)  8.79 us
    all_to_all x1, starting transfers between devices, body(): lax.all_to_all(attached, 'ulysses', split_axis=0, concat_axis=0, tiled=True)  5.97 us
  transfers between devices with their start and end apart: 6, of which 6 were waited for; matrix products, arithmetic and copies ran while one was open for 3% of the time, Pallas kernels for 2%

profile of v3, /device:TPU:1, one launch (start us, length us, event | category | flops | bytes accessed | tf_op | source)
XLA Modules:
  0.0 227.6 jit_solution(17235104958978917774)
XLA Ops:
  0.6 1.5 convert_reduce_fusion
  2.2 0.2 convert_reduce_fusion.2
  2.4 0.6 select_reduce_fusion.1.heads_ref
  3.0 4.9 %pack_heads.1 = bf16[32,4,128,128]{3,2,1,0:T(8,128)(2,1)} custom-call(s32[32]{0:T(128)} %select_reduce_fusion.1.heads_ref, bf16[128,3072]{1,0:T(8,128)(2,1)} %bitcast.22, bf16[128,3072]{1,0:T(8,128)(2,1)} %bitcast.23, bf16[128,3072]{1,0:T(8,128)(2,1)} %bitcast.24, bf16[128,3072]{1,0:T(8,128)(2,1)} %bitcast.25), custom_call_target="tpu_custom_call" | custom-call | tf_op jit(solution)/shard_map/pack_heads/pallas_call | solution.py:60
  7.8 0.0 copy-start
  7.8 0.0 copy-start.2
  7.9 0.0 copy-start.3
  7.9 8.8 %all-to-all-start = ((bf16[32,4,128,128]{3,2,1,0:T(8,128)(2,1)}), bf16[32,4,128,128]{3,2,1,0:T(8,128)(2,1)}, u32[]{:S(2)}, u32[]{:S(2)}) async-start(bf16[32,4,128,128]{3,2,1,0:T(8,128)(2,1)} %pack_heads.1), calls=%async_computation | async-start | bytes 8388608 | tf_op jit(solution)/shard_map/all_to_all | solution.py:436
  16.7 0.0 copy-done
  16.7 0.6 dynamic_slice.8
  19.2 0.7 broadcast_compare_fusion
  20.0 0.2 multiply_reduce_fusion
  20.2 0.4 select_reduce_fusion
  20.6 0.7 add.56.list_ref
  21.3 0.1 convert_reduce_fusion.1
  21.4 0.6 reduce_max.29
  22.7 0.0 copy-done.2
  22.7 0.6 abs_reduce_fusion.1
  23.9 0.0 copy-done.3
  23.9 0.6 abs_reduce_fusion
  25.2 0.7 reshape.76.mask_ref
  25.9 0.6 concatenate.3.info_ref
  26.4 0.6 pad_maximum_fusion.gain_ref
  27.0 39.9 %all-to-all-done.hbm_ref = bf16[32,4,128,128]{3,2,1,0:T(8,128)(2,1)} async-done(((bf16[32,4,128,128]{3,2,1,0:T(8,128)(2,1)}), bf16[32,4,128,128]{3,2,1,0:T(8,128)(2,1)}, u32[]{:S(2)}, u32[]{:S(2)}) %all-to-all-start) | async-done | bytes 4194336 | tf_op jit(solution)/shard_map/all_to_all | solution.py:436
  66.9 96.4 %item_grads.1 = (bf16[32,2,128,128]{3,2,1,0:T(8,128)(2,1)}, bf16[32,128,128]{2,1,0:T(8,128)(2,1)}, f32[16,128]{1,0:T(8,128)}) custom-call(s32[40]{0:T(128)} %concatenate.3.info_ref, s32[1024]{0:T(1024)} %add.56.list_ref, s32[1024]{0:T(1024)} %reshape.76.mask_ref, f32[2,128]{1,0:T(2,128)} %pad_maximum_fusion.gain_ref, ...), custom_call_target="tpu_custom_call" | custom-call | tf_op jit(solution)/shard_map/item_grads/pallas_call | solution.py:292
  163.4 0.0 copy-start.1
  163.4 10.6 %all-to-all-start.1 = ((bf16[32,256,128]{2,1,0:T(8,128)(2,1)}), bf16[32,256,128]{2,1,0:T(8,128)(2,1)S(1)}, u32[]{:S(2)}, u32[]{:S(2)}) async-start(bf16[32,256,128]{2,1,0:T(8,128)(2,1)} %bitcast.21), calls=%async_computation.1 | async-start | bytes 4194304 | tf_op jit(solution)/shard_map/all_to_all | solution.py:452
  174.0 0.0 copy-done.1
  174.0 1.7 collective-permute-start
  175.7 1.3 collective-permute-done
  177.0 3.0 %collective-permute-start.1 = (f32[2,128]{1,0:T(2,128)S(1)}, f32[2,128]{1,0:T(2,128)S(1)}, u32[]{:S(2)}, u32[]{:S(2)}) collective-permute-start(f32[2,128]{1,0:T(2,128)S(1)} %add.57), channel_id=1, source_target_pairs={{0,64},{32,96},{64,0},{96,32},{128,192},{160,224},{192,128},{224,1... | collective-permute-start | bytes 3080 | tf_op jit(solution)/shard_map/ppermute | solution.py:398
  180.0 1.3 collective-permute-done.1
  181.3 6.1 %collective-permute-start.2 = (f32[2,128]{1,0:T(2,128)S(1)}, f32[2,128]{1,0:T(2,128)S(1)}, u32[]{:S(2)}, u32[]{:S(2)}) collective-permute-start(f32[2,128]{1,0:T(2,128)S(1)} %add.58), channel_id=1, source_target_pairs={{0,128},{32,160},{64,192},{96,224},{128,0},{160,32},{192,64},{224,... | collective-permute-start | bytes 3080 | tf_op jit(solution)/shard_map/ppermute | solution.py:398
  187.4 1.3 collective-permute-done.2
  188.6 0.6 add.59.part_ref
  189.2 2.5 %attach_gains.1 = bf16[32,144,128]{2,1,0:T(8,128)(2,1)} custom-call(f32[2,128]{1,0:T(2,128)} %add.59.part_ref, bf16[32,128,128]{2,1,0:T(8,128)(2,1)} %get-tuple-element.14.v_ref), custom_call_target="tpu_custom_call" | custom-call | tf_op jit(solution)/shard_map/attach_gains/pallas_call | solution.py:385
  191.6 10.3 %all-to-all-done.1.in_ref = bf16[32,256,128]{2,1,0:T(8,128)(2,1)S(1)} async-done(((bf16[32,256,128]{2,1,0:T(8,128)(2,1)}), bf16[32,256,128]{2,1,0:T(8,128)(2,1)S(1)}, u32[]{:S(2)}, u32[]{:S(2)}) %all-to-all-start.1) | async-done | bytes 2097184 | tf_op jit(solution)/shard_map/all_to_all | solution.py:452
  202.0 6.0 %all-to-all-start.2 = ((bf16[32,144,128]{2,1,0:T(8,128)(2,1)}), bf16[32,144,128]{2,1,0:T(8,128)(2,1)S(1)}, u32[]{:S(2)}, u32[]{:S(2)}) async-start(bf16[32,144,128]{2,1,0:T(8,128)(2,1)} %attach_gains.1), calls=%async_computation.2 | async-start | bytes 2359296 | tf_op jit(solution)/shard_map/all_to_all | solution.py:457
  207.9 2.2 merge_heads.2
  210.1 15.6 %all-to-all-done.2.in_ref = bf16[32,144,128]{2,1,0:T(8,128)(2,1)S(1)} async-done(((bf16[32,144,128]{2,1,0:T(8,128)(2,1)}), bf16[32,144,128]{2,1,0:T(8,128)(2,1)S(1)}, u32[]{:S(2)}, u32[]{:S(2)}) %all-to-all-start.2) | async-done | bytes 1179680 | tf_op jit(solution)/shard_map/all_to_all | solution.py:457
  225.7 1.9 merge_heads.3
  (9 shorter events, 0.0 us)
Async XLA Ops:
  7.8 8.8 %copy-start = (s32[32]{0:T(128)S(1)}, s32[32]{0:T(128)}, u32[]{:S(2)}) copy-start(s32[32]{0:T(128)} %select_reduce_fusion.1.heads_ref) | copy-start | bytes 388
  7.8 14.8 %copy-start.2 = (f32[128]{0:T(128)S(1)}, f32[128]{0:T(128)}, u32[]{:S(2)}) copy-start(f32[128]{0:T(128)} %param.11) | copy-start | bytes 1540
  7.9 16.1 %copy-start.3 = (f32[128]{0:T(128)S(1)}, f32[128]{0:T(128)}, u32[]{:S(2)}) copy-start(f32[128]{0:T(128)} %param.12) | copy-start | bytes 1540
  7.9 59.1 %all-to-all-start = ((bf16[32,4,128,128]{3,2,1,0:T(8,128)(2,1)}), bf16[32,4,128,128]{3,2,1,0:T(8,128)(2,1)}, u32[]{:S(2)}, u32[]{:S(2)}) async-start(bf16[32,4,128,128]{3,2,1,0:T(8,128)(2,1)} %pack_heads.1), calls=%async_computation | async-start | bytes 8388608 | tf_op jit(solution)/shard_map/all_to_all | solution.py:436
  163.4 10.7 %copy-start.1 = (f32[16,128]{1,0:T(8,128)S(1)}, f32[16,128]{1,0:T(8,128)}, u32[]{:S(2)}) copy-start(f32[16,128]{1,0:T(8,128)} %get-tuple-element.13) | copy-start | bytes 24580
  163.4 38.6 %all-to-all-start.1 = ((bf16[32,256,128]{2,1,0:T(8,128)(2,1)}), bf16[32,256,128]{2,1,0:T(8,128)(2,1)S(1)}, u32[]{:S(2)}, u32[]{:S(2)}) async-start(bf16[32,256,128]{2,1,0:T(8,128)(2,1)} %bitcast.21), calls=%async_computation.1 | async-start | bytes 4194304 | tf_op jit(solution)/shard_map/all_to_all | solution.py:452
  174.0 3.0 %collective-permute-start = (f32[2,128]{1,0:T(2,128)S(1)}, f32[2,128]{1,0:T(2,128)S(1)}, u32[]{:S(2)}, u32[]{:S(2)}) collective-permute-start(f32[2,128]{1,0:T(2,128)S(1)} %bitcast_reduce_fusion), channel_id=1, source_target_pairs={{0,32},{32,0},{64,96},{96,64},{128,160},{160,128},{192,224},{224,1... | collective-permute-start | bytes 3080 | tf_op jit(solution)/shard_map/ppermute | solution.py:398
  177.0 4.2 %collective-permute-start.1 = (f32[2,128]{1,0:T(2,128)S(1)}, f32[2,128]{1,0:T(2,128)S(1)}, u32[]{:S(2)}, u32[]{:S(2)}) collective-permute-start(f32[2,128]{1,0:T(2,128)S(1)} %add.57), channel_id=1, source_target_pairs={{0,64},{32,96},{64,0},{96,32},{128,192},{160,224},{192,128},{224,1... | collective-permute-start | bytes 3080 | tf_op jit(solution)/shard_map/ppermute | solution.py:398
  181.3 7.4 %collective-permute-start.2 = (f32[2,128]{1,0:T(2,128)S(1)}, f32[2,128]{1,0:T(2,128)S(1)}, u32[]{:S(2)}, u32[]{:S(2)}) collective-permute-start(f32[2,128]{1,0:T(2,128)S(1)} %add.58), channel_id=1, source_target_pairs={{0,128},{32,160},{64,192},{96,224},{128,0},{160,32},{192,64},{224,... | collective-permute-start | bytes 3080 | tf_op jit(solution)/shard_map/ppermute | solution.py:398
  202.0 23.8 %all-to-all-start.2 = ((bf16[32,144,128]{2,1,0:T(8,128)(2,1)}), bf16[32,144,128]{2,1,0:T(8,128)(2,1)S(1)}, u32[]{:S(2)}, u32[]{:S(2)}) async-start(bf16[32,144,128]{2,1,0:T(8,128)(2,1)} %attach_gains.1), calls=%async_computation.2 | async-start | bytes 2359296 | tf_op jit(solution)/shard_map/all_to_all | solution.py:457

commit v4 on v3

--- a/solution.py
+++ b/solution.py
@@ -124,27 +124,37 @@
             kt[j] = normed.T
             acc[j] = jnp.zeros((BLOCK, 2 * HEAD_DIM), F32)
             qk_out[j, 0] = zero_half
+            shifts[j] = jnp.zeros((8, BLOCK), F32)
         return carry
+
+    def prepare_query(i, padded):
+        raw = in_ref[i, 0].astype(F32)
+        normed = (raw * inv_spread(raw) * q_gain).astype(BF16)
+        o_block = in_ref[i, 3]
+        left[i, :HEAD_DIM, :BLOCK] = normed.T
+        left[i, HEAD_DIM:, BLOCK:] = o_block.T
+        right[i, :BLOCK, :HEAD_DIM] = o_block
+        right[i, BLOCK:, HEAD_DIM:] = normed
+        if padded:
+            left[i, :HEAD_DIM, BLOCK:] = zero_half
+            left[i, HEAD_DIM:, :BLOCK] = zero_half
+            right[i, :BLOCK, HEAD_DIM:] = zero_half
+            right[i, BLOCK:, :HEAD_DIM] = zero_half
 
     def prepare_queries(step, carry):
         for u in range(UNROLL):
-            i = first + step * UNROLL + u
-            raw = in_ref[i, 0].astype(F32)
-            normed = (raw * inv_spread(raw) * q_gain).astype(BF16)
-            o_block = in_ref[i, 3]
-            left[i, :HEAD_DIM, :BLOCK] = normed.T
-            left[i, HEAD_DIM:, BLOCK:] = o_block.T
-            left[i, :HEAD_DIM, BLOCK:] = zero_half
-            left[i, HEAD_DIM:, :BLOCK] = zero_half
-            right[i, :BLOCK, :HEAD_DIM] = o_block
-            right[i, BLOCK:, HEAD_DIM:] = normed
-            right[i, :BLOCK, HEAD_DIM:] = zero_half
-            right[i, BLOCK:, :HEAD_DIM] = zero_half
-            shifts[i] = jnp.zeros((8, BLOCK), F32)
+            prepare_query(first + step * UNROLL + u, True)
         return carry
 
+    def finish_query(i, total_qt):
+        grad, gains = norm_back(in_ref[i, 0].astype(F32), q_gain, total_qt.T * SCALE)
+        qk_out[i, 0] = grad.astype(BF16)
+        return fold_rows(gains)
+
     lax.fori_loop(0, nb // UNROLL, prepare_keys, 0)
-    lax.fori_loop(0, (last - first) // UNROLL, prepare_queries, 0)
+    dense = info_ref[3]
+    ahead = jnp.where((dense == 0) | (careful > 0), last - first, 0)
+    lax.fori_loop(0, ahead // UNROLL, prepare_queries, 0)
     kv[nb] = jnp.zeros((BLOCK, 2 * HEAD_DIM), BF16)
     kt[nb] = zero_half
     acc[nb] = jnp.zeros((BLOCK, 2 * HEAD_DIM), F32)
@@ -173,7 +183,7 @@
             weights = jnp.exp2(both[:, :BLOCK] * SCORE2 + (jnp.where(allowed, 0.0, NEG_FILL) - shift))
             grads = both[:, BLOCK:]
             pairs[at, :, :BLOCK] = weights
-            pairs[at, :, BLOCK:] = grads
+            pairs[at, :, BLOCK : 2 * BLOCK] = grads
             total = total + fold_rows(weights)
             dotted = dotted + fold_rows(weights * grads)
         return total, dotted
@@ -182,7 +192,7 @@
         halves, keys = [], []
         for at, j, _ in places:
             weights = pairs[at, :, :BLOCK] * inv_total
-            half = (weights * (pairs[at, :, BLOCK:] - row_delta)).astype(BF16)
+            half = (weights * (pairs[at, :, BLOCK : 2 * BLOCK] - row_delta)).astype(BF16)
             acc[j] += jnp.dot(
                 jnp.concatenate([weights.astype(BF16), half], axis=1), right[i], preferred_element_type=F32
             )
@@ -200,32 +210,74 @@
         inv_total = 1.0 / jnp.sum(total, axis=0, keepdims=True)
         return inv_total, jnp.sum(dotted, axis=0, keepdims=True) * inv_total
 
-    def rows_in_turn(stats, query_block):
-        def two_blocks(step, stats):
-            i = first + 2 * step
-            stats = query_block(i, i + 1, pairs_even, pairs_odd, stats)
-            return query_block(i + 1, jnp.minimum(i + 2, last - 1), pairs_odd, pairs_even, stats)
-
-        lax.fori_loop(0, (last - first) // 2, two_blocks, stats)
+    def in_turn(start, stop, stats, visit):
+        def two_visits(step, stats):
+            i = start + 2 * step
+            stats = visit(i, i + 1, pairs_even, pairs_odd, stats)
+            return visit(i + 1, jnp.minimum(i + 2, stop - 1), pairs_odd, pairs_even, stats)
+
+        lax.fori_loop(0, (stop - start) // 2, two_visits, stats)
 
     def attend_all():
-        def places(i):
-            return [(j, j, mask_ref[i * nb + j] > 0) for j in range(nb)]
-
-        def query_block(i, later, mine, other, stats):
+        wide = 2 * BLOCK
+        earlier = lax.broadcasted_iota(jnp.int32, (1, wide), 1) < BLOCK
+        top, low = slice(0, BLOCK), slice(BLOCK, wide)
+
+        def score_two(pairs, two):
+            i = 2 * two
+            queries = jnp.concatenate([left[i, top, top], left[i + 1, top, top]], axis=1)
+            outs = jnp.concatenate([left[i, low, low], left[i + 1, low, low]], axis=1)
+            shift = jnp.concatenate([shifts[i, 0:1, :], shifts[i + 1, 0:1, :]], axis=1)
+            total = dotted = jnp.zeros((8, wide), F32)
+            for j in range(nb):
+                scores = jnp.dot(kv[j, :, :HEAD_DIM], queries, preferred_element_type=F32)
+                grads = jnp.dot(kv[j, :, HEAD_DIM:], outs, preferred_element_type=F32)
+                bias = jnp.where(
+                    earlier,
+                    jnp.where(mask_ref[i * nb + j] > 0, 0.0, NEG_FILL),
+                    jnp.where(mask_ref[(i + 1) * nb + j] > 0, 0.0, NEG_FILL),
+                )
+                weights = jnp.exp2(scores * SCORE2 + (bias - shift))
+                pairs[j, :, :wide] = weights
+                pairs[j, :, wide:] = grads
+                total = total + fold_rows(weights)
+                dotted = dotted + fold_rows(weights * grads)
+            return total, dotted
+
+        def visit(two, later, mine, other, stats):
+            i = 2 * two
+            for u in range(2):
+                prepare_query(2 * later + u, False)
             inv_total, row_delta = row_scales(stats)
-            grad_qt[i] = grad_group(mine, i, places(i), inv_total, row_delta, no_grad)
-            return score_group(other, later, places(later), (zero, zero))
-
-        rows_in_turn(score_group(pairs_even, first, places(first), (zero, zero)), query_block)
+            outs = jnp.concatenate([right[i, top, top], right[i + 1, top, top]], axis=0)
+            queries = jnp.concatenate([right[i, low, low], right[i + 1, low, low]], axis=0)
+            halves = []
+            for j in range(nb):
+                weights = mine[j, :, :wide] * inv_total
+                half = (weights * (mine[j, :, wide:] - row_delta)).astype(BF16)
+                acc[j, :, :HEAD_DIM] += jnp.dot(weights.astype(BF16), outs, preferred_element_type=F32)
+                acc[j, :, HEAD_DIM:] += jnp.dot(half, queries, preferred_element_type=F32)
+                halves.append(half)
+            total_qt = jnp.dot(
+                jnp.concatenate([kt[j] for j in range(nb)], axis=1),
+                jnp.concatenate(halves, axis=0),
+                preferred_element_type=F32,
+            )
+            stats = score_two(other, later)
+            part_ref[0:8, :] += finish_query(i, total_qt[:, :BLOCK]) + finish_query(i + 1, total_qt[:, BLOCK:])
+            return stats
+
+        for u in range(2):
+            prepare_query(first + u, False)
+        in_turn(first // 2, last // 2, score_two(pairs_even, first // 2), visit)
 
     def attend_listed():
         def clear(at, carry):
-            pairs_even[at] = jnp.zeros((BLOCK, 2 * BLOCK), F32)
-            pairs_odd[at] = jnp.zeros((BLOCK, 2 * BLOCK), F32)
+            pairs_even[at, :, : 2 * BLOCK] = jnp.zeros((BLOCK, 2 * BLOCK), F32)
+            pairs_odd[at, :, : 2 * BLOCK] = jnp.zeros((BLOCK, 2 * BLOCK), F32)
             return carry
 
-        lax.fori_loop(0, slots, clear, 0)
+        lax.fori_loop(0, 2 * GROUP + DENSE_FROM, clear, 0)
 
         def groups_of(i):
             return (info_ref[8 + i] + (GROUP - 1)) // GROUP
@@ -251,18 +303,15 @@
         stats = lax.fori_loop(
             0, groups_of(first), lambda g, s: score_group(pairs_even, first, places(first, g), s), (zero, zero)
         )
-        rows_in_turn(stats, query_block)
-
-    dense = info_ref[3]
+        in_turn(first, last, stats, query_block)
+
     pl.when(dense > 0)(attend_all)
     pl.when(dense == 0)(attend_listed)
 
     def finish_queries(step, total):
         for u in range(UNROLL):
             i = first + step * UNROLL + u
-            grad, gains = norm_back(in_ref[i, 0].astype(F32), q_gain, grad_qt[i].T * SCALE)
-            qk_out[i, 0] = grad.astype(BF16)
-            total = total + fold_rows(gains)
+            total = total + finish_query(i, grad_qt[i])
         return total
 
     def finish_keys(step, total):
@@ -276,7 +325,8 @@
             copy.start()
         return total
 
-    part_ref[0:8, :] = lax.fori_loop(0, (last - first) // UNROLL, finish_queries, zero)
+    behind = jnp.where(dense == 0, last - first, 0)
+    part_ref[0:8, :] += lax.fori_loop(0, behind // UNROLL, finish_queries, zero)
     part_ref[8:16, :] = lax.fori_loop(0, nb // UNROLL, finish_keys, zero)
     for step in range(nb // UNROLL):
         for copy in store(step):
@@ -307,8 +357,8 @@
             pltpu.SemaphoreType.DMA((nb // UNROLL,)),
             pltpu.VMEM((nb + 1, BLOCK, 2 * HEAD_DIM), BF16),
             pltpu.VMEM((nb + 1, HEAD_DIM, BLOCK), BF16),
-            pltpu.VMEM((slots, BLOCK, 2 * BLOCK), F32),
-            pltpu.VMEM((slots, BLOCK, 2 * BLOCK), F32),
+            pltpu.VMEM((slots, BLOCK, 4 * BLOCK), F32),
+            pltpu.VMEM((slots, BLOCK, 4 * BLOCK), F32),
             pltpu.VMEM((nb + 1, BLOCK, 2 * HEAD_DIM), F32),
             pltpu.VMEM((nb, 2 * HEAD_DIM, 2 * BLOCK), BF16),
             pltpu.VMEM((nb, 2 * BLOCK, 2 * HEAD_DIM), BF16),

time: 227 us -> 221 us (0.974)
  Pallas kernels: 108 us -> 103 us
  starting transfers between devices: 36.2 us -> 33.5 us
    pallas_call x1, Pallas kernels: 96.4 us -> 92.1 us  [item_grads(): pl.pallas_call(functools.partial(item_kernel, nb), out_shape=(jax.ShapeDt...]
    all_to_all x1, starting transfers between devices: 10.6 us -> 7.91 us  [body(): lax.all_to_all(grads_qk.reshape(nb, 2 * BLOCK, HEAD_DIM), 'ulysses', spli...]
where the time goes in v4:
time: 221 us
  Pallas kernels  103 us (47%)
  waiting for transfers between devices  69.6 us (31%)
  starting transfers between devices  33.5 us (15%)
  other arithmetic  6.76 us (3%)
  between operations  4.71 us (2%)
  local copies, waits for them, and re-layouts  2.52 us (1%)
    pallas_call x1, Pallas kernels, item_grads(): pl.pallas_call(functools.partial(item_kernel, nb), out_shape=(jax.ShapeDt...  92.1 us
    all_to_all x1, waiting for transfers between devices, body(): lax.all_to_all(outgoing, 'ulysses', split_axis=0, concat_axis=0, tiled=True)  39.9 us
    all_to_all x1, waiting for transfers between devices, body(): lax.all_to_all(attached, 'ulysses', split_axis=0, concat_axis=0, tiled=True)  15.6 us
    ppermute x3, starting transfers between devices, sum_over_videos(): lax.ppermute(part, 'dp', [(i, i ^ step) for i in range(count)])  10.8 us
    all_to_all x1, waiting for transfers between devices, body(): lax.all_to_all(grads_qk.reshape(nb, 2 * BLOCK, HEAD_DIM), 'ulysses', spli...  10.3 us
    all_to_all x1, starting transfers between devices, body(): lax.all_to_all(outgoing, 'ulysses', split_axis=0, concat_axis=0, tiled=True)  8.79 us
    all_to_all x1, starting transfers between devices, body(): lax.all_to_all(grads_qk.reshape(nb, 2 * BLOCK, HEAD_DIM), 'ulysses', spli...  7.91 us
    all_to_all x1, starting transfers between devices, body(): lax.all_to_all(attached, 'ulysses', split_axis=0, concat_axis=0, tiled=True)  5.97 us
  transfers between devices with their start and end apart: 6, of which 6 were waited for; matrix products, arithmetic and copies ran while one was open for 3% of the time, Pallas kernels for 2%

profile of v4, /device:TPU:1, one launch (start us, length us, event | category | flops | bytes accessed | tf_op | source)
XLA Modules:
  0.0 220.6 jit_solution(10477164957839008775)
XLA Ops:
  0.6 1.5 convert_reduce_fusion
  2.2 0.2 convert_reduce_fusion.2
  2.4 0.6 select_reduce_fusion.1.heads_ref
  3.0 4.9 %pack_heads.1 = bf16[32,4,128,128]{3,2,1,0:T(8,128)(2,1)} custom-call(s32[32]{0:T(128)} %select_reduce_fusion.1.heads_ref, bf16[128,3072]{1,0:T(8,128)(2,1)} %bitcast.22, bf16[128,3072]{1,0:T(8,128)(2,1)} %bitcast.23, bf16[128,3072]{1,0:T(8,128)(2,1)} %bitcast.24, bf16[128,3072]{1,0:T(8,128)(2,1)} %bitcast.25), custom_call_target="tpu_custom_call" | custom-call | tf_op jit(solution)/shard_map/pack_heads/pallas_call | solution.py:60
  7.8 0.0 copy-start
  7.8 0.0 copy-start.2
  7.9 0.0 copy-start.3
  7.9 8.8 %all-to-all-start = ((bf16[32,4,128,128]{3,2,1,0:T(8,128)(2,1)}), bf16[32,4,128,128]{3,2,1,0:T(8,128)(2,1)}, u32[]{:S(2)}, u32[]{:S(2)}) async-start(bf16[32,4,128,128]{3,2,1,0:T(8,128)(2,1)} %pack_heads.1), calls=%async_computation | async-start | bytes 8388608 | tf_op jit(solution)/shard_map/all_to_all | solution.py:486
  16.7 0.0 copy-done
  16.7 0.6 dynamic_slice.8
  19.2 0.7 broadcast_compare_fusion
  20.0 0.2 multiply_reduce_fusion
  20.2 0.4 select_reduce_fusion
  20.6 0.7 add.56.list_ref
  21.3 0.1 convert_reduce_fusion.1
  21.4 0.6 reduce_max.29
  22.7 0.0 copy-done.2
  22.7 0.6 abs_reduce_fusion.1
  23.9 0.0 copy-done.3
  23.9 0.6 abs_reduce_fusion
  25.2 0.7 reshape.76.mask_ref
  25.9 0.6 concatenate.3.info_ref
  26.4 0.6 pad_maximum_fusion.gain_ref
  27.0 39.9 %all-to-all-done.hbm_ref = bf16[32,4,128,128]{3,2,1,0:T(8,128)(2,1)} async-done(((bf16[32,4,128,128]{3,2,1,0:T(8,128)(2,1)}), bf16[32,4,128,128]{3,2,1,0:T(8,128)(2,1)}, u32[]{:S(2)}, u32[]{:S(2)}) %all-to-all-start) | async-done | bytes 4194336 | tf_op jit(solution)/shard_map/all_to_all | solution.py:486
  66.9 92.1 %item_grads.1 = (bf16[32,2,128,128]{3,2,1,0:T(8,128)(2,1)}, bf16[32,128,128]{2,1,0:T(8,128)(2,1)}, f32[16,128]{1,0:T(8,128)}) custom-call(s32[40]{0:T(128)} %concatenate.3.info_ref, s32[1024]{0:T(1024)} %add.56.list_ref, s32[1024]{0:T(1024)} %reshape.76.mask_ref, f32[2,128]{1,0:T(2,128)} %pad_maximum_fusion.gain_ref, ...), custom_call_target="tpu_custom_call" | custom-call | tf_op jit(solution)/shard_map/item_grads/pallas_call | solution.py:342
  159.1 0.0 copy-start.1
  159.1 7.9 %all-to-all-start.1 = ((bf16[32,256,128]{2,1,0:T(8,128)(2,1)}), bf16[32,256,128]{2,1,0:T(8,128)(2,1)S(1)}, u32[]{:S(2)}, u32[]{:S(2)}) async-start(bf16[32,256,128]{2,1,0:T(8,128)(2,1)} %bitcast.21), calls=%async_computation.1 | async-start | bytes 4194304 | tf_op jit(solution)/shard_map/all_to_all | solution.py:502
  167.0 0.0 copy-done.1
  167.0 1.7 collective-permute-start
  168.7 1.3 collective-permute-done
  170.0 3.0 %collective-permute-start.1 = (f32[2,128]{1,0:T(2,128)S(1)}, f32[2,128]{1,0:T(2,128)S(1)}, u32[]{:S(2)}, u32[]{:S(2)}) collective-permute-start(f32[2,128]{1,0:T(2,128)S(1)} %add.57), channel_id=1, source_target_pairs={{0,64},{32,96},{64,0},{96,32},{128,192},{160,224},{192,128},{224,1... | collective-permute-start | bytes 3080 | tf_op jit(solution)/shard_map/ppermute | solution.py:448
  173.0 1.3 collective-permute-done.1
  174.2 6.1 %collective-permute-start.2 = (f32[2,128]{1,0:T(2,128)S(1)}, f32[2,128]{1,0:T(2,128)S(1)}, u32[]{:S(2)}, u32[]{:S(2)}) collective-permute-start(f32[2,128]{1,0:T(2,128)S(1)} %add.58), channel_id=1, source_target_pairs={{0,128},{32,160},{64,192},{96,224},{128,0},{160,32},{192,64},{224,... | collective-permute-start | bytes 3080 | tf_op jit(solution)/shard_map/ppermute | solution.py:448
  180.4 1.3 collective-permute-done.2
  181.6 0.6 add.59.part_ref
  182.2 2.5 %attach_gains.1 = bf16[32,144,128]{2,1,0:T(8,128)(2,1)} custom-call(f32[2,128]{1,0:T(2,128)} %add.59.part_ref, bf16[32,128,128]{2,1,0:T(8,128)(2,1)} %get-tuple-element.14.v_ref), custom_call_target="tpu_custom_call" | custom-call | tf_op jit(solution)/shard_map/attach_gains/pallas_call | solution.py:435
  184.6 10.3 %all-to-all-done.1.in_ref = bf16[32,256,128]{2,1,0:T(8,128)(2,1)S(1)} async-done(((bf16[32,256,128]{2,1,0:T(8,128)(2,1)}), bf16[32,256,128]{2,1,0:T(8,128)(2,1)S(1)}, u32[]{:S(2)}, u32[]{:S(2)}) %all-to-all-start.1) | async-done | bytes 2097184 | tf_op jit(solution)/shard_map/all_to_all | solution.py:502
  194.9 6.0 %all-to-all-start.2 = ((bf16[32,144,128]{2,1,0:T(8,128)(2,1)}), bf16[32,144,128]{2,1,0:T(8,128)(2,1)S(1)}, u32[]{:S(2)}, u32[]{:S(2)}) async-start(bf16[32,144,128]{2,1,0:T(8,128)(2,1)} %attach_gains.1), calls=%async_computation.2 | async-start | bytes 2359296 | tf_op jit(solution)/shard_map/all_to_all | solution.py:507
  200.9 2.2 merge_heads.2
  203.1 15.6 %all-to-all-done.2.in_ref = bf16[32,144,128]{2,1,0:T(8,128)(2,1)S(1)} async-done(((bf16[32,144,128]{2,1,0:T(8,128)(2,1)}), bf16[32,144,128]{2,1,0:T(8,128)(2,1)S(1)}, u32[]{:S(2)}, u32[]{:S(2)}) %all-to-all-start.2) | async-done | bytes 1179680 | tf_op jit(solution)/shard_map/all_to_all | solution.py:507
  218.7 1.9 merge_heads.3
  (9 shorter events, 0.0 us)
Async XLA Ops:
  7.8 8.8 %copy-start = (s32[32]{0:T(128)S(1)}, s32[32]{0:T(128)}, u32[]{:S(2)}) copy-start(s32[32]{0:T(128)} %select_reduce_fusion.1.heads_ref) | copy-start | bytes 388
  7.8 14.8 %copy-start.2 = (f32[128]{0:T(128)S(1)}, f32[128]{0:T(128)}, u32[]{:S(2)}) copy-start(f32[128]{0:T(128)} %param.11) | copy-start | bytes 1540
  7.9 16.1 %copy-start.3 = (f32[128]{0:T(128)S(1)}, f32[128]{0:T(128)}, u32[]{:S(2)}) copy-start(f32[128]{0:T(128)} %param.12) | copy-start | bytes 1540
  7.9 59.1 %all-to-all-start = ((bf16[32,4,128,128]{3,2,1,0:T(8,128)(2,1)}), bf16[32,4,128,128]{3,2,1,0:T(8,128)(2,1)}, u32[]{:S(2)}, u32[]{:S(2)}) async-start(bf16[32,4,128,128]{3,2,1,0:T(8,128)(2,1)} %pack_heads.1), calls=%async_computation | async-start | bytes 8388608 | tf_op jit(solution)/shard_map/all_to_all | solution.py:486
  159.1 7.9 %copy-start.1 = (f32[16,128]{1,0:T(8,128)S(1)}, f32[16,128]{1,0:T(8,128)}, u32[]{:S(2)}) copy-start(f32[16,128]{1,0:T(8,128)} %get-tuple-element.13) | copy-start | bytes 24580
  159.1 35.9 %all-to-all-start.1 = ((bf16[32,256,128]{2,1,0:T(8,128)(2,1)}), bf16[32,256,128]{2,1,0:T(8,128)(2,1)S(1)}, u32[]{:S(2)}, u32[]{:S(2)}) async-start(bf16[32,256,128]{2,1,0:T(8,128)(2,1)} %bitcast.21), calls=%async_computation.1 | async-start | bytes 4194304 | tf_op jit(solution)/shard_map/all_to_all | solution.py:502
  167.0 3.0 %collective-permute-start = (f32[2,128]{1,0:T(2,128)S(1)}, f32[2,128]{1,0:T(2,128)S(1)}, u32[]{:S(2)}, u32[]{:S(2)}) collective-permute-start(f32[2,128]{1,0:T(2,128)S(1)} %bitcast_reduce_fusion), channel_id=1, source_target_pairs={{0,32},{32,0},{64,96},{96,64},{128,160},{160,128},{192,224},{224,1... | collective-permute-start | bytes 3080 | tf_op jit(solution)/shard_map/ppermute | solution.py:448
  170.0 4.2 %collective-permute-start.1 = (f32[2,128]{1,0:T(2,128)S(1)}, f32[2,128]{1,0:T(2,128)S(1)}, u32[]{:S(2)}, u32[]{:S(2)}) collective-permute-start(f32[2,128]{1,0:T(2,128)S(1)} %add.57), channel_id=1, source_target_pairs={{0,64},{32,96},{64,0},{96,32},{128,192},{160,224},{192,128},{224,1... | collective-permute-start | bytes 3080 | tf_op jit(solution)/shard_map/ppermute | solution.py:448
  174.2 7.4 %collective-permute-start.2 = (f32[2,128]{1,0:T(2,128)S(1)}, f32[2,128]{1,0:T(2,128)S(1)}, u32[]{:S(2)}, u32[]{:S(2)}) collective-permute-start(f32[2,128]{1,0:T(2,128)S(1)} %add.58), channel_id=1, source_target_pairs={{0,128},{32,160},{64,192},{96,224},{128,0},{160,32},{192,64},{224,... | collective-permute-start | bytes 3080 | tf_op jit(solution)/shard_map/ppermute | solution.py:448
  194.9 23.8 %all-to-all-start.2 = ((bf16[32,144,128]{2,1,0:T(8,128)(2,1)}), bf16[32,144,128]{2,1,0:T(8,128)(2,1)S(1)}, u32[]{:S(2)}, u32[]{:S(2)}) async-start(bf16[32,144,128]{2,1,0:T(8,128)(2,1)} %attach_gains.1), calls=%async_computation.2 | async-start | bytes 2359296 | tf_op jit(solution)/shard_map/all_to_all | solution.py:507

commit v5 on v4

--- a/solution.py
+++ b/solution.py
@@ -27,7 +27,23 @@
 BF16 = jnp.bfloat16
 
 
-def pack_kernel(heads_ref, q_ref, k_ref, v_ref, o_ref, out_ref, wide, tall, in_sems, out_sems):
+def plan_items(mask):
+    on = jnp.where(mask > 0, 1.0, 0.0)
+    totals = jnp.sum(jnp.sum(on, axis=1), axis=1, keepdims=True)
+    shape = (HEADS, HEAD_DIM)
+    head = lax.broadcasted_iota(jnp.int32, shape, 0)
+    lane = lax.broadcasted_iota(jnp.int32, shape, 1)
+    across = jnp.sum(jnp.where(head == lane, totals, 0.0), axis=0, keepdims=True)
+    ahead = (across > totals) | ((across == totals) & (lane < head))
+    rank = jnp.sum(jnp.where(ahead & (lane < HEADS), 1.0, 0.0), axis=1, keepdims=True)
+    wanted = jnp.where(lane < 2 * SPLITS, lane >> 1, lane - SPLITS).astype(F32)
+    return jnp.sum(jnp.where(rank == wanted, head.astype(F32), 0.0), axis=0, keepdims=True).astype(jnp.int32)
+
+
+def pack_kernel(
+    mask_ref, q_ref, k_ref, v_ref, o_ref, out_ref, plan_ref,
+    wide, tall, heads_ref, in_sems, out_sems, plan_sem,
+):
     rows = q_ref.shape[0]
     part = rows // CHUNK
     loads, stores = [], []
@@ -37,12 +53,16 @@
             copy = pltpu.make_async_copy(src.at[at], wide.at[which, at], in_sems.at[which, c])
             copy.start()
             loads.append(copy)
+    plan_ref[...] = jnp.broadcast_to(plan_items(mask_ref[...]), plan_ref.shape)
+    copy = pltpu.make_async_copy(plan_ref, heads_ref, plan_sem)
+    copy.start()
+    copy.wait()
     for which in range(4):
         for c in range(CHUNK):
             loads[which * CHUNK + c].wait()
 
         def move(slot, carry, which=which):
-            at = pl.multiple_of(heads_ref[slot] * HEAD_DIM, HEAD_DIM)
+            at = pl.multiple_of(heads_ref[0, slot] * HEAD_DIM, HEAD_DIM)
             tall[which, slot] = wide[which, :, pl.ds(at, HEAD_DIM)]
             return carry
 
@@ -54,23 +74,29 @@
         copy.wait()
 
 
-def pack(item_heads, q_raw, k_raw, values, grad_out):
+def pack(block_masks, q_raw, k_raw, values, grad_out):
     rows, width = q_raw.shape
+    vmem = pl.BlockSpec(memory_space=pltpu.VMEM)
     hbm = pl.BlockSpec(memory_space=pltpu.HBM)
     return pl.pallas_call(
         pack_kernel,
-        out_shape=jax.ShapeDtypeStruct((ITEMS, 4, rows, HEAD_DIM), BF16),
-        in_specs=[pl.BlockSpec(memory_space=pltpu.SMEM)] + [hbm] * 4,
-        out_specs=hbm,
+        out_shape=(
+            jax.ShapeDtypeStruct((ITEMS, 4, rows, HEAD_DIM), BF16),
+            jax.ShapeDtypeStruct((8, HEAD_DIM), jnp.int32),
+        ),
+        in_specs=[vmem] + [hbm] * 4,
+        out_specs=(hbm, vmem),
         scratch_shapes=[
             pltpu.VMEM((4, rows, width), BF16),
             pltpu.VMEM((4, ITEMS, rows, HEAD_DIM), BF16),
+            pltpu.SMEM((8, HEAD_DIM), jnp.int32),
             pltpu.SemaphoreType.DMA((4, CHUNK)),
             pltpu.SemaphoreType.DMA((4,)),
+            pltpu.SemaphoreType.DMA,
         ],
         compiler_params=pltpu.CompilerParams(vmem_limit_bytes=60 * 2**20),
         name="pack_heads",
-    )(item_heads, q_raw, k_raw, values, grad_out)
+    )(block_masks, q_raw, k_raw, values, grad_out)
 
 
 def inv_spread(raw_float):
@@ -145,6 +171,19 @@
         for u in range(UNROLL):
             prepare_query(first + step * UNROLL + u, True)
         return carry
+
+    def finish_key(j):
+        grad, gains = norm_back(in_ref[j, 1].astype(F32), k_gain, acc[j, :, HEAD_DIM:] * SCALE)
+        qk_out[j, 1] = grad.astype(BF16)
+        v_out[j] = acc[j, :, :HEAD_DIM].astype(BF16)
+        return fold_rows(gains)
+
+    def finish_keys(step, total):
+        for u in range(UNROLL):
+            total = total + finish_key(step * UNROLL + u)
+        for copy in store(step):
+            copy.start()
+        return total
 
     def finish_query(i, total_qt):
         grad, gains = norm_back(in_ref[i, 0].astype(F32), q_gain, total_qt.T * SCALE)
@@ -244,10 +283,8 @@
                 dotted = dotted + fold_rows(weights * grads)
             return total, dotted
 
-        def visit(two, later, mine, other, stats):
+        def grads_of_two(mine, two, stats):
             i = 2 * two
-            for u in range(2):
-                prepare_query(2 * later + u, False)
             inv_total, row_delta = row_scales(stats)
             outs = jnp.concatenate([right[i, top, top], right[i + 1, top, top]], axis=0)
             queries = jnp.concatenate([right[i, low, low], right[i + 1, low, low]], axis=0)
@@ -258,18 +295,40 @@
                 acc[j, :, :HEAD_DIM] += jnp.dot(weights.astype(BF16), outs, preferred_element_type=F32)
                 acc[j, :, HEAD_DIM:] += jnp.dot(half, queries, preferred_element_type=F32)
                 halves.append(half)
-            total_qt = jnp.dot(
+            return jnp.dot(
                 jnp.concatenate([kt[j] for j in range(nb)], axis=1),
                 jnp.concatenate(halves, axis=0),
                 preferred_element_type=F32,
             )
-            stats = score_two(other, later)
-            part_ref[0:8, :] += finish_query(i, total_qt[:, :BLOCK]) + finish_query(i + 1, total_qt[:, BLOCK:])
+
+        def finish_two(two, total_qt):
+            part_ref[0:8, :] += finish_query(2 * two, total_qt[:, :BLOCK]) + finish_query(
+                2 * two + 1, total_qt[:, BLOCK:]
+            )
+
+        def visit(two, mine, other, stats):
+            for u in range(2):
+                prepare_query(2 * two + 2 + u, False)
+            total_qt = grads_of_two(mine, two, stats)
+            stats = score_two(other, two + 1)
+            finish_two(two, total_qt)
             return stats
 
         for u in range(2):
             prepare_query(first + u, False)
-        in_turn(first // 2, last // 2, score_two(pairs_even, first // 2), visit)
+        start, stop = first // 2, last // 2
+
+        def two_visits(step, stats):
+            stats = visit(start + 2 * step, pairs_even, pairs_odd, stats)
+            return visit(start + 2 * step + 1, pairs_odd, pairs_even, stats)
+
+        stats = lax.fori_loop(0, (stop - start) // 2 - 1, two_visits, score_two(pairs_even, start))
+        stats = visit(stop - 2, pairs_even, pairs_odd, stats)
+        finish_two(stop - 1, grads_of_two(pairs_odd, stop - 1, stats))
+        total = zero
+        for step in range(nb // UNROLL):
+            total = finish_keys(step, total)
+        part_ref[8:16, :] += total
 
     def attend_listed():
         def clear(at, carry):
@@ -314,20 +373,9 @@
             total = total + finish_query(i, grad_qt[i])
         return total
 
-    def finish_keys(step, total):
-        for u in range(UNROLL):
-            j = step * UNROLL + u
-            grad, gains = norm_back(in_ref[j, 1].astype(F32), k_gain, acc[j, :, HEAD_DIM:] * SCALE)
-            qk_out[j, 1] = grad.astype(BF16)
-            v_out[j] = acc[j, :, :HEAD_DIM].astype(BF16)
-            total = total + fold_rows(gains)
-        for copy in store(step):
-            copy.start()
-        return total
-
     behind = jnp.where(dense == 0, last - first, 0)
     part_ref[0:8, :] += lax.fori_loop(0, behind // UNROLL, finish_queries, zero)
-    part_ref[8:16, :] = lax.fori_loop(0, nb // UNROLL, finish_keys, zero)
+    part_ref[8:16, :] += lax.fori_loop(0, jnp.where(dense == 0, nb // UNROLL, 0), finish_keys, zero)
     for step in range(nb // UNROLL):
         for copy in store(step):
             copy.wait()
@@ -450,18 +498,6 @@
     return part
 
 
-def plan_items(block_masks):
-    totals = jnp.sum((block_masks > 0).astype(jnp.int32), axis=(1, 2))
-    heads = jnp.arange(HEADS, dtype=jnp.int32)
-    ahead = (totals[None, :] > totals[:, None]) | (
-        (totals[None, :] == totals[:, None]) & (heads[None, :] < heads[:, None])
-    )
-    rank = jnp.sum(ahead.astype(jnp.int32), axis=1)
-    counter = jnp.arange(ITEMS, dtype=jnp.int32)
-    wanted = jnp.where(counter < 2 * SPLITS, counter // 2, counter - SPLITS)
-    return jnp.sum(jnp.where(rank[None, :] == wanted[:, None], heads[None, :], 0), axis=1)
-
-
 def block_lists(mask_head):
     nb = mask_head.shape[0]
     on = (mask_head > 0).astype(jnp.int32)
@@ -481,8 +517,8 @@
     nb = block_masks.shape[1]
     seq_len = tok_rows * lax.axis_size("ulysses")
     videos = lax.axis_size("dp")
-    item_heads = plan_items(block_masks)
-    outgoing = pack(item_heads, q_raw[0], k_raw[0], values[0], grad_out[0])
+    outgoing, plan = pack(block_masks, q_raw[0], k_raw[0], values[0], grad_out[0])
+    item_heads = plan[0, :ITEMS]
     arrived = lax.all_to_all(outgoing, "ulysses", split_axis=0, concat_axis=0, tiled=True)
     head = lax.dynamic_index_in_dim(item_heads, device_rank, 0, keepdims=False)
     mask_head = lax.dynamic_index_in_dim(block_masks, head, 0, keepdims=False)

time: 221 us -> 219 us (level)
  Pallas kernels: 103 us -> 106 us
  starting transfers between devices: 33.5 us -> 30.5 us
  other arithmetic: 6.76 us -> 4.43 us
    all_to_all x1, starting transfers between devices: 7.91 us -> 5.05 us  [body(): lax.all_to_all(grads_qk.reshape(nb, 2 * BLOCK, HEAD_DIM), 'ulysses', spli...]
    reduce_sum x3 -> x0, other arithmetic: 2.32 us -> none  [the longest x1 1.53 us: plan_items(): totals = jnp.sum((block_masks > 0).astype(jnp.int32), axis=(1, 2))]
where the time goes in v5:
time: 219 us; the launch traced here: 218 us
  Pallas kernels  106 us (48%)
  waiting for transfers between devices  69 us (32%)
  starting transfers between devices  30.5 us (14%)
  between operations  4.7 us (2%)
  other arithmetic  4.43 us (2%)
  local copies, waits for them, and re-layouts  3.2 us (1%)
    pallas_call x1, Pallas kernels, item_grads(): pl.pallas_call(functools.partial(item_kernel, nb), out_shape=(jax.ShapeDt...  93.7 us
    all_to_all x1, waiting for transfers between devices, body(): lax.all_to_all(outgoing, 'ulysses', split_axis=0, concat_axis=0, tiled=True)  39.3 us
    all_to_all x1, waiting for transfers between devices, body(): lax.all_to_all(attached, 'ulysses', split_axis=0, concat_axis=0, tiled=True)  15.6 us
    ppermute x3, starting transfers between devices, sum_over_videos(): lax.ppermute(part, 'dp', [(i, i ^ step) for i in range(count)])  10.8 us
    all_to_all x1, waiting for transfers between devices, body(): lax.all_to_all(grads_qk.reshape(nb, 2 * BLOCK, HEAD_DIM), 'ulysses', spli...  10.3 us
    all_to_all x1, starting transfers between devices, body(): lax.all_to_all(outgoing, 'ulysses', split_axis=0, concat_axis=0, tiled=True)  8.66 us
    all_to_all x1, starting transfers between devices, body(): lax.all_to_all(attached, 'ulysses', split_axis=0, concat_axis=0, tiled=True)  5.97 us
    pallas_call x1, Pallas kernels, pack(): pl.pallas_call(pack_kernel, out_shape=(jax.ShapeDtypeStruct((ITEMS, 4, ro...  5.8 us
  transfers between devices with their start and end apart: 6, of which 6 were waited for; matrix products, arithmetic and copies ran while one was open for 3% of the time, Pallas kernels for 2%

profile of v5, /device:TPU:1, one launch (start us, length us, event | category | flops | bytes accessed | tf_op | source)
XLA Modules:
  0.0 217.7 jit_solution(3043720539431090908)
XLA Ops:
  0.6 5.8 %pack_heads.1 = (bf16[32,4,128,128]{3,2,1,0:T(8,128)(2,1)}, s32[8,128]{1,0:T(8,128)}) custom-call(s32[24,32,32]{2,1,0:T(8,128)} %mask_ref.1, bf16[128,3072]{1,0:T(8,128)(2,1)} %bitcast.24, bf16[128,3072]{1,0:T(8,128)(2,1)} %bitcast.25, bf16[128,3072]{1,0:T(8,128)(2,1)} %bitcast.26, bf16[128,3072]{1,0:T(8,128)(2,1)} %bitcast.27), custom_call_target="tpu_custom_call" | custom-call | tf_op jit(solution)/shard_map/pack_heads/pallas_call | solution.py:81
  6.4 0.0 copy-start.1
  6.5 0.0 copy-start.2
  6.5 8.7 %all-to-all-start = ((bf16[32,4,128,128]{3,2,1,0:T(8,128)(2,1)}), bf16[32,4,128,128]{3,2,1,0:T(8,128)(2,1)}, u32[]{:S(2)}, u32[]{:S(2)}) async-start(bf16[32,4,128,128]{3,2,1,0:T(8,128)(2,1)} %get-tuple-element.16), calls=%async_computation | async-start | bytes 8388608 | tf_op jit(solution)/shard_map/all_to_all | solution.py:522
  15.1 0.7 fusion.2
  15.8 0.6 constant_dynamic-slice_fusion.1
  18.4 0.7 broadcast_compare_fusion
  19.1 0.2 multiply_reduce_fusion
  19.4 0.4 select_reduce_fusion
  19.7 0.7 add.46.list_ref
  20.4 0.1 convert_reduce_fusion
  20.5 0.6 reduce_max.29
  21.8 0.0 copy-done.1
  21.8 0.6 abs_reduce_fusion.1
  23.1 0.0 copy-done.2
  23.1 0.6 abs_reduce_fusion
  24.3 0.7 reshape.57.mask_ref
  25.0 0.6 concatenate.3.info_ref
  25.6 0.6 pad_maximum_fusion.gain_ref
  26.1 39.3 %all-to-all-done.hbm_ref = bf16[32,4,128,128]{3,2,1,0:T(8,128)(2,1)} async-done(((bf16[32,4,128,128]{3,2,1,0:T(8,128)(2,1)}), bf16[32,4,128,128]{3,2,1,0:T(8,128)(2,1)}, u32[]{:S(2)}, u32[]{:S(2)}) %all-to-all-start) | async-done | bytes 4194336 | tf_op jit(solution)/shard_map/all_to_all | solution.py:522
  65.4 93.7 %item_grads.1 = (bf16[32,2,128,128]{3,2,1,0:T(8,128)(2,1)}, bf16[32,128,128]{2,1,0:T(8,128)(2,1)}, f32[16,128]{1,0:T(8,128)}) custom-call(s32[40]{0:T(128)} %concatenate.3.info_ref, s32[1024]{0:T(1024)} %add.46.list_ref, s32[1024]{0:T(1024)} %reshape.57.mask_ref, f32[2,128]{1,0:T(2,128)} %pad_maximum_fusion.gain_ref, ...), custom_call_target="tpu_custom_call" | custom-call | tf_op jit(solution)/shard_map/item_grads/pallas_call | solution.py:390
  159.1 0.0 copy-start
  159.1 5.0 %all-to-all-start.1 = ((bf16[32,256,128]{2,1,0:T(8,128)(2,1)}), bf16[32,256,128]{2,1,0:T(8,128)(2,1)S(1)}, u32[]{:S(2)}, u32[]{:S(2)}) async-start(bf16[32,256,128]{2,1,0:T(8,128)(2,1)} %bitcast.23), calls=%async_computation.1 | async-start | bytes 4194304 | tf_op jit(solution)/shard_map/all_to_all | solution.py:538
  164.1 0.0 copy-done
  164.2 1.7 collective-permute-start
  165.9 1.3 collective-permute-done
  167.1 3.0 %collective-permute-start.1 = (f32[2,128]{1,0:T(2,128)S(1)}, f32[2,128]{1,0:T(2,128)S(1)}, u32[]{:S(2)}, u32[]{:S(2)}) collective-permute-start(f32[2,128]{1,0:T(2,128)S(1)} %add.47), channel_id=1, source_target_pairs={{0,64},{32,96},{64,0},{96,32},{128,192},{160,224},{192,128},{224,1... | collective-permute-start | bytes 3080 | tf_op jit(solution)/shard_map/ppermute | solution.py:496
  170.1 1.3 collective-permute-done.1
  171.4 6.1 %collective-permute-start.2 = (f32[2,128]{1,0:T(2,128)S(1)}, f32[2,128]{1,0:T(2,128)S(1)}, u32[]{:S(2)}, u32[]{:S(2)}) collective-permute-start(f32[2,128]{1,0:T(2,128)S(1)} %add.48), channel_id=1, source_target_pairs={{0,128},{32,160},{64,192},{96,224},{128,0},{160,32},{192,64},{224,... | collective-permute-start | bytes 3080 | tf_op jit(solution)/shard_map/ppermute | solution.py:496
  177.5 1.3 collective-permute-done.2
  178.7 0.6 add.49.part_ref
  179.3 2.5 %attach_gains.1 = bf16[32,144,128]{2,1,0:T(8,128)(2,1)} custom-call(f32[2,128]{1,0:T(2,128)} %add.49.part_ref, bf16[32,128,128]{2,1,0:T(8,128)(2,1)} %get-tuple-element.18.v_ref), custom_call_target="tpu_custom_call" | custom-call | tf_op jit(solution)/shard_map/attach_gains/pallas_call | solution.py:483
  181.8 10.3 %all-to-all-done.1.in_ref = bf16[32,256,128]{2,1,0:T(8,128)(2,1)S(1)} async-done(((bf16[32,256,128]{2,1,0:T(8,128)(2,1)}), bf16[32,256,128]{2,1,0:T(8,128)(2,1)S(1)}, u32[]{:S(2)}, u32[]{:S(2)}) %all-to-all-start.1) | async-done | bytes 2097184 | tf_op jit(solution)/shard_map/all_to_all | solution.py:538
  192.1 6.0 %all-to-all-start.2 = ((bf16[32,144,128]{2,1,0:T(8,128)(2,1)}), bf16[32,144,128]{2,1,0:T(8,128)(2,1)S(1)}, u32[]{:S(2)}, u32[]{:S(2)}) async-start(bf16[32,144,128]{2,1,0:T(8,128)(2,1)} %attach_gains.1), calls=%async_computation.2 | async-start | bytes 2359296 | tf_op jit(solution)/shard_map/all_to_all | solution.py:543
  198.1 2.2 %merge_heads.2 = (bf16[128,3072]{1,0:T(8,128)(2,1)}, bf16[128,3072]{1,0:T(8,128)(2,1)}) custom-call(s32[32]{0:T(128)S(1)} %get-tuple-element.30.heads_ref, bf16[32,256,128]{2,1,0:T(8,128)(2,1)S(1)} %all-to-all-done.1.in_ref), custom_call_target="tpu_custom_call" | custom-call | tf_op jit(solution)/shard_map/merge_heads/pallas_call | solution.py:454
  200.2 15.6 %all-to-all-done.2.in_ref = bf16[32,144,128]{2,1,0:T(8,128)(2,1)S(1)} async-done(((bf16[32,144,128]{2,1,0:T(8,128)(2,1)}), bf16[32,144,128]{2,1,0:T(8,128)(2,1)S(1)}, u32[]{:S(2)}, u32[]{:S(2)}) %all-to-all-start.2) | async-done | bytes 1179680 | tf_op jit(solution)/shard_map/all_to_all | solution.py:543
  215.9 1.9 merge_heads.3
  (8 shorter events, 0.0 us)
Async XLA Ops:
  6.4 15.4 %copy-start.1 = (f32[128]{0:T(128)S(1)}, f32[128]{0:T(128)}, u32[]{:S(2)}) copy-start(f32[128]{0:T(128)} %param.11) | copy-start | bytes 1540
  6.5 16.6 %copy-start.2 = (f32[128]{0:T(128)S(1)}, f32[128]{0:T(128)}, u32[]{:S(2)}) copy-start(f32[128]{0:T(128)} %param.12) | copy-start | bytes 1540
  6.5 58.9 %all-to-all-start = ((bf16[32,4,128,128]{3,2,1,0:T(8,128)(2,1)}), bf16[32,4,128,128]{3,2,1,0:T(8,128)(2,1)}, u32[]{:S(2)}, u32[]{:S(2)}) async-start(bf16[32,4,128,128]{3,2,1,0:T(8,128)(2,1)} %get-tuple-element.16), calls=%async_computation | async-start | bytes 8388608 | tf_op jit(solution)/shard_map/all_to_all | solution.py:522
  159.1 5.1 %copy-start = (f32[16,128]{1,0:T(8,128)S(1)}, f32[16,128]{1,0:T(8,128)}, u32[]{:S(2)}) copy-start(f32[16,128]{1,0:T(8,128)} %get-tuple-element.17) | copy-start | bytes 24580
  159.1 33.0 %all-to-all-start.1 = ((bf16[32,256,128]{2,1,0:T(8,128)(2,1)}), bf16[32,256,128]{2,1,0:T(8,128)(2,1)S(1)}, u32[]{:S(2)}, u32[]{:S(2)}) async-start(bf16[32,256,128]{2,1,0:T(8,128)(2,1)} %bitcast.23), calls=%async_computation.1 | async-start | bytes 4194304 | tf_op jit(solution)/shard_map/all_to_all | solution.py:538
  164.2 3.0 %collective-permute-start = (f32[2,128]{1,0:T(2,128)S(1)}, f32[2,128]{1,0:T(2,128)S(1)}, u32[]{:S(2)}, u32[]{:S(2)}) collective-permute-start(f32[2,128]{1,0:T(2,128)S(1)} %bitcast_reduce_fusion), channel_id=1, source_target_pairs={{0,32},{32,0},{64,96},{96,64},{128,160},{160,128},{192,224},{224,1... | collective-permute-start | bytes 3080 | tf_op jit(solution)/shard_map/ppermute | solution.py:496
  167.1 4.2 %collective-permute-start.1 = (f32[2,128]{1,0:T(2,128)S(1)}, f32[2,128]{1,0:T(2,128)S(1)}, u32[]{:S(2)}, u32[]{:S(2)}) collective-permute-start(f32[2,128]{1,0:T(2,128)S(1)} %add.47), channel_id=1, source_target_pairs={{0,64},{32,96},{64,0},{96,32},{128,192},{160,224},{192,128},{224,1... | collective-permute-start | bytes 3080 | tf_op jit(solution)/shard_map/ppermute | solution.py:496
  171.4 7.4 %collective-permute-start.2 = (f32[2,128]{1,0:T(2,128)S(1)}, f32[2,128]{1,0:T(2,128)S(1)}, u32[]{:S(2)}, u32[]{:S(2)}) collective-permute-start(f32[2,128]{1,0:T(2,128)S(1)} %add.48), channel_id=1, source_target_pairs={{0,128},{32,160},{64,192},{96,224},{128,0},{160,32},{192,64},{224,... | collective-permute-start | bytes 3080 | tf_op jit(solution)/shard_map/ppermute | solution.py:496
  192.1 23.8 %all-to-all-start.2 = ((bf16[32,144,128]{2,1,0:T(8,128)(2,1)}), bf16[32,144,128]{2,1,0:T(8,128)(2,1)S(1)}, u32[]{:S(2)}, u32[]{:S(2)}) async-start(bf16[32,144,128]{2,1,0:T(8,128)(2,1)} %attach_gains.1), calls=%async_computation.2 | async-start | bytes 2359296 | tf_op jit(solution)/shard_map/all_to_all | solution.py:543

commit v6 on v5

--- a/solution.py
+++ b/solution.py
@@ -14,8 +14,8 @@
 ITEMS = 32
 GROUP = 5
 DENSE_FROM = 12
-CHUNK = 4
-UNROLL = 4
+CHUNK = 1
+UNROLL = 8
 
 NORM_EPS = 1e-06
 NEG_FILL = -1e30
@@ -66,7 +66,7 @@
             tall[which, slot] = wide[which, :, pl.ds(at, HEAD_DIM)]
             return carry
 
-        lax.fori_loop(0, ITEMS, move, 0)
+        lax.fori_loop(0, ITEMS, move, 0, unroll=4)
         copy = pltpu.make_async_copy(tall.at[which], out_ref.at[:, which], out_sems.at[which])
         copy.start()
         stores.append(copy)
@@ -437,13 +437,13 @@
             out[:, pl.ds(at, HEAD_DIM)] = piece(slot, which)
         return carry
 
-    lax.fori_loop(0, SPLITS, pair, 0)
-    lax.fori_loop(2 * SPLITS, ITEMS, single, 0)
+    lax.fori_loop(0, SPLITS, pair, 0, unroll=4)
+    lax.fori_loop(2 * SPLITS, ITEMS, single, 0, unroll=4)
     if len(out_refs) > count:
         def tail(slot, total):
             return total + in_ref[slot, count * BLOCK : count * BLOCK + 16, :].astype(F32)
 
-        total = lax.fori_loop(0, ITEMS, tail, jnp.zeros((16, HEAD_DIM), F32))
+        total = lax.fori_loop(0, ITEMS, tail, jnp.zeros((16, HEAD_DIM), F32), unroll=8)
         out_refs[count][...] = (total[0:2] + (total[2:4] + total[4:6])) * tail_scale
 
 

time: 219 us -> 218 us (level)
  Pallas kernels: 106 us -> 103 us
  starting transfers between devices: 30.5 us -> 33.1 us
    all_to_all x1, starting transfers between devices: 5.05 us -> 7.62 us  [body(): lax.all_to_all(grads_qk.reshape(nb, 2 * BLOCK, HEAD_DIM), 'ulysses', spli...]
    pallas_call x1, Pallas kernels: 93.7 us -> 91.2 us  [item_grads(): pl.pallas_call(functools.partial(item_kernel, nb), out_shape=(jax.ShapeDt...]
  transfers between devices with their start and end apart: 6 -> 6, of which waited for: 6 -> 6; matrix products, arithmetic and copies ran while one was open for 3% -> 4% of each run, Pallas kernels for 2% -> 2%
where the time goes in v6:
time: 218 us; the launch traced here: 217 us
  Pallas kernels  103 us (47%)
  waiting for transfers between devices  69 us (32%)
  starting transfers between devices  33.1 us (15%)
  between operations  4.7 us (2%)
  other arithmetic  4.43 us (2%)
  local copies, waits for them, and re-layouts  3.2 us (1%)
    pallas_call x1, Pallas kernels, item_grads(): pl.pallas_call(functools.partial(item_kernel, nb), out_shape=(jax.ShapeDt...  91.2 us
    all_to_all x1, waiting for transfers between devices, body(): lax.all_to_all(outgoing, 'ulysses', split_axis=0, concat_axis=0, tiled=True)  39.3 us
    all_to_all x1, waiting for transfers between devices, body(): lax.all_to_all(attached, 'ulysses', split_axis=0, concat_axis=0, tiled=True)  15.7 us
    ppermute x3, starting transfers between devices, sum_over_videos(): lax.ppermute(part, 'dp', [(i, i ^ step) for i in range(count)])  10.8 us
    all_to_all x1, waiting for transfers between devices, body(): lax.all_to_all(grads_qk.reshape(nb, 2 * BLOCK, HEAD_DIM), 'ulysses', spli...  10.3 us
    all_to_all x1, starting transfers between devices, body(): lax.all_to_all(outgoing, 'ulysses', split_axis=0, concat_axis=0, tiled=True)  8.66 us
    all_to_all x1, starting transfers between devices, body(): lax.all_to_all(grads_qk.reshape(nb, 2 * BLOCK, HEAD_DIM), 'ulysses', spli...  7.62 us
    all_to_all x1, starting transfers between devices, body(): lax.all_to_all(attached, 'ulysses', split_axis=0, concat_axis=0, tiled=True)  5.97 us
  transfers between devices with their start and end apart: 6, of which 6 were waited for; matrix products, arithmetic and copies ran while one was open for 4% of the time, Pallas kernels for 2%

profile of v6, /device:TPU:1, one launch (start us, length us, event | category | flops | bytes accessed | tf_op | source)
XLA Modules:
  0.0 217.0 jit_solution(13492274841598000730)
XLA Ops:
  0.6 5.1 %pack_heads.1 = (bf16[32,4,128,128]{3,2,1,0:T(8,128)(2,1)}, s32[8,128]{1,0:T(8,128)}) custom-call(s32[24,32,32]{2,1,0:T(8,128)} %mask_ref.1, bf16[128,3072]{1,0:T(8,128)(2,1)} %bitcast.24, bf16[128,3072]{1,0:T(8,128)(2,1)} %bitcast.25, bf16[128,3072]{1,0:T(8,128)(2,1)} %bitcast.26, bf16[128,3072]{1,0:T(8,128)(2,1)} %bitcast.27), custom_call_target="tpu_custom_call" | custom-call | tf_op jit(solution)/shard_map/pack_heads/pallas_call | solution.py:81
  5.8 0.0 copy-start.1
  5.8 0.0 copy-start.2
  5.8 8.7 %all-to-all-start = ((bf16[32,4,128,128]{3,2,1,0:T(8,128)(2,1)}), bf16[32,4,128,128]{3,2,1,0:T(8,128)(2,1)}, u32[]{:S(2)}, u32[]{:S(2)}) async-start(bf16[32,4,128,128]{3,2,1,0:T(8,128)(2,1)} %get-tuple-element.16), calls=%async_computation | async-start | bytes 8388608 | tf_op jit(solution)/shard_map/all_to_all | solution.py:522
  14.5 0.7 fusion.2
  15.2 0.6 constant_dynamic-slice_fusion.1
  17.7 0.7 broadcast_compare_fusion
  18.5 0.2 multiply_reduce_fusion
  18.7 0.4 select_reduce_fusion
  19.1 0.7 add.46.list_ref
  19.7 0.1 convert_reduce_fusion
  19.8 0.6 reduce_max.29
  21.1 0.0 copy-done.1
  21.1 0.6 abs_reduce_fusion.1
  22.4 0.0 copy-done.2
  22.4 0.6 abs_reduce_fusion
  23.7 0.7 reshape.57.mask_ref
  24.3 0.6 concatenate.3.info_ref
  24.9 0.6 pad_maximum_fusion.gain_ref
  25.5 39.3 %all-to-all-done.hbm_ref = bf16[32,4,128,128]{3,2,1,0:T(8,128)(2,1)} async-done(((bf16[32,4,128,128]{3,2,1,0:T(8,128)(2,1)}), bf16[32,4,128,128]{3,2,1,0:T(8,128)(2,1)}, u32[]{:S(2)}, u32[]{:S(2)}) %all-to-all-start) | async-done | bytes 4194336 | tf_op jit(solution)/shard_map/all_to_all | solution.py:522
  64.7 91.2 %item_grads.1 = (bf16[32,2,128,128]{3,2,1,0:T(8,128)(2,1)}, bf16[32,128,128]{2,1,0:T(8,128)(2,1)}, f32[16,128]{1,0:T(8,128)}) custom-call(s32[40]{0:T(128)} %concatenate.3.info_ref, s32[1024]{0:T(1024)} %add.46.list_ref, s32[1024]{0:T(1024)} %reshape.57.mask_ref, f32[2,128]{1,0:T(2,128)} %pad_maximum_fusion.gain_ref, ...), custom_call_target="tpu_custom_call" | custom-call | tf_op jit(solution)/shard_map/item_grads/pallas_call | solution.py:390
  155.9 0.0 copy-start
  155.9 7.6 %all-to-all-start.1 = ((bf16[32,256,128]{2,1,0:T(8,128)(2,1)}), bf16[32,256,128]{2,1,0:T(8,128)(2,1)S(1)}, u32[]{:S(2)}, u32[]{:S(2)}) async-start(bf16[32,256,128]{2,1,0:T(8,128)(2,1)} %bitcast.23), calls=%async_computation.1 | async-start | bytes 4194304 | tf_op jit(solution)/shard_map/all_to_all | solution.py:538
  163.5 0.0 copy-done
  163.6 1.7 collective-permute-start
  165.3 1.3 collective-permute-done
  166.5 3.0 %collective-permute-start.1 = (f32[2,128]{1,0:T(2,128)S(1)}, f32[2,128]{1,0:T(2,128)S(1)}, u32[]{:S(2)}, u32[]{:S(2)}) collective-permute-start(f32[2,128]{1,0:T(2,128)S(1)} %add.47), channel_id=1, source_target_pairs={{0,64},{32,96},{64,0},{96,32},{128,192},{160,224},{192,128},{224,1... | collective-permute-start | bytes 3080 | tf_op jit(solution)/shard_map/ppermute | solution.py:496
  169.5 1.3 collective-permute-done.1
  170.8 6.1 %collective-permute-start.2 = (f32[2,128]{1,0:T(2,128)S(1)}, f32[2,128]{1,0:T(2,128)S(1)}, u32[]{:S(2)}, u32[]{:S(2)}) collective-permute-start(f32[2,128]{1,0:T(2,128)S(1)} %add.48), channel_id=1, source_target_pairs={{0,128},{32,160},{64,192},{96,224},{128,0},{160,32},{192,64},{224,... | collective-permute-start | bytes 3080 | tf_op jit(solution)/shard_map/ppermute | solution.py:496
  176.9 1.3 collective-permute-done.2
  178.1 0.6 add.49.part_ref
  178.7 2.5 %attach_gains.1 = bf16[32,144,128]{2,1,0:T(8,128)(2,1)} custom-call(f32[2,128]{1,0:T(2,128)} %add.49.part_ref, bf16[32,128,128]{2,1,0:T(8,128)(2,1)} %get-tuple-element.18.v_ref), custom_call_target="tpu_custom_call" | custom-call | tf_op jit(solution)/shard_map/attach_gains/pallas_call | solution.py:483
  181.2 10.3 %all-to-all-done.1.in_ref = bf16[32,256,128]{2,1,0:T(8,128)(2,1)S(1)} async-done(((bf16[32,256,128]{2,1,0:T(8,128)(2,1)}), bf16[32,256,128]{2,1,0:T(8,128)(2,1)S(1)}, u32[]{:S(2)}, u32[]{:S(2)}) %all-to-all-start.1) | async-done | bytes 2097184 | tf_op jit(solution)/shard_map/all_to_all | solution.py:538
  191.5 6.0 %all-to-all-start.2 = ((bf16[32,144,128]{2,1,0:T(8,128)(2,1)}), bf16[32,144,128]{2,1,0:T(8,128)(2,1)S(1)}, u32[]{:S(2)}, u32[]{:S(2)}) async-start(bf16[32,144,128]{2,1,0:T(8,128)(2,1)} %attach_gains.1), calls=%async_computation.2 | async-start | bytes 2359296 | tf_op jit(solution)/shard_map/all_to_all | solution.py:543
  197.5 2.1 merge_heads.2
  199.6 15.7 %all-to-all-done.2.in_ref = bf16[32,144,128]{2,1,0:T(8,128)(2,1)S(1)} async-done(((bf16[32,144,128]{2,1,0:T(8,128)(2,1)}), bf16[32,144,128]{2,1,0:T(8,128)(2,1)S(1)}, u32[]{:S(2)}, u32[]{:S(2)}) %all-to-all-start.2) | async-done | bytes 1179680 | tf_op jit(solution)/shard_map/all_to_all | solution.py:543
  215.3 1.7 merge_heads.3
  (8 shorter events, 0.0 us)
Async XLA Ops:
  5.8 15.4 %copy-start.1 = (f32[128]{0:T(128)S(1)}, f32[128]{0:T(128)}, u32[]{:S(2)}) copy-start(f32[128]{0:T(128)} %param.11) | copy-start | bytes 1540
  5.8 16.6 %copy-start.2 = (f32[128]{0:T(128)S(1)}, f32[128]{0:T(128)}, u32[]{:S(2)}) copy-start(f32[128]{0:T(128)} %param.12) | copy-start | bytes 1540
  5.8 58.9 %all-to-all-start = ((bf16[32,4,128,128]{3,2,1,0:T(8,128)(2,1)}), bf16[32,4,128,128]{3,2,1,0:T(8,128)(2,1)}, u32[]{:S(2)}, u32[]{:S(2)}) async-start(bf16[32,4,128,128]{3,2,1,0:T(8,128)(2,1)} %get-tuple-element.16), calls=%async_computation | async-start | bytes 8388608 | tf_op jit(solution)/shard_map/all_to_all | solution.py:522
  155.9 7.6 %copy-start = (f32[16,128]{1,0:T(8,128)S(1)}, f32[16,128]{1,0:T(8,128)}, u32[]{:S(2)}) copy-start(f32[16,128]{1,0:T(8,128)} %get-tuple-element.17) | copy-start | bytes 24580
  155.9 35.6 %all-to-all-start.1 = ((bf16[32,256,128]{2,1,0:T(8,128)(2,1)}), bf16[32,256,128]{2,1,0:T(8,128)(2,1)S(1)}, u32[]{:S(2)}, u32[]{:S(2)}) async-start(bf16[32,256,128]{2,1,0:T(8,128)(2,1)} %bitcast.23), calls=%async_computation.1 | async-start | bytes 4194304 | tf_op jit(solution)/shard_map/all_to_all | solution.py:538
  163.6 3.0 %collective-permute-start = (f32[2,128]{1,0:T(2,128)S(1)}, f32[2,128]{1,0:T(2,128)S(1)}, u32[]{:S(2)}, u32[]{:S(2)}) collective-permute-start(f32[2,128]{1,0:T(2,128)S(1)} %bitcast_reduce_fusion), channel_id=1, source_target_pairs={{0,32},{32,0},{64,96},{96,64},{128,160},{160,128},{192,224},{224,1... | collective-permute-start | bytes 3080 | tf_op jit(solution)/shard_map/ppermute | solution.py:496
  166.5 4.2 %collective-permute-start.1 = (f32[2,128]{1,0:T(2,128)S(1)}, f32[2,128]{1,0:T(2,128)S(1)}, u32[]{:S(2)}, u32[]{:S(2)}) collective-permute-start(f32[2,128]{1,0:T(2,128)S(1)} %add.47), channel_id=1, source_target_pairs={{0,64},{32,96},{64,0},{96,32},{128,192},{160,224},{192,128},{224,1... | collective-permute-start | bytes 3080 | tf_op jit(solution)/shard_map/ppermute | solution.py:496
  170.8 7.4 %collective-permute-start.2 = (f32[2,128]{1,0:T(2,128)S(1)}, f32[2,128]{1,0:T(2,128)S(1)}, u32[]{:S(2)}, u32[]{:S(2)}) collective-permute-start(f32[2,128]{1,0:T(2,128)S(1)} %add.48), channel_id=1, source_target_pairs={{0,128},{32,160},{64,192},{96,224},{128,0},{160,32},{192,64},{224,... | collective-permute-start | bytes 3080 | tf_op jit(solution)/shard_map/ppermute | solution.py:496
  191.5 23.8 %all-to-all-start.2 = ((bf16[32,144,128]{2,1,0:T(8,128)(2,1)}), bf16[32,144,128]{2,1,0:T(8,128)(2,1)S(1)}, u32[]{:S(2)}, u32[]{:S(2)}) async-start(bf16[32,144,128]{2,1,0:T(8,128)(2,1)} %attach_gains.1), calls=%async_computation.2 | async-start | bytes 2359296 | tf_op jit(solution)/shard_map/all_to_all | solution.py:543
